TPU v7x, 512 devices: a whole 4x8x8 slice. The times are simulated.
512 devices in a mesh: site: 16 (over y, core), sector: 32 (over z, x).
Axes of the slice: x: 4, y: 8, z: 8, core: 2. Of those that a mesh axis runs over, the one named last changes fastest.
Arguments:
- mps: bfloat16 [64, 64, 64, 256], P('sector', 'site'), may hold values from -0.75 to 0.75
- left_env: bfloat16 [32, 64, 64, 1088], P('sector', 'site'), may hold values from -6 to 6
- right_env: bfloat16 [32, 64, 64, 1088], P('sector', 'site'), may hold values from -6 to 6
- row_fill: int32 [64, 64], P('sector', 'site'), may hold values from 32 to 64
- col_fill: int32 [64, 64, 4], P('sector', 'site'), may hold values from 32 to 64
- mpo_values: bfloat16 [17, 17, 4], replicated, may hold values from -1.5 to 1.5
- mpo_pattern: int32 [17, 17, 4], replicated, may hold values 0 or 1
Outputs:
- lanczos_vector: float32 [64, 64, 64, 256], P('sector', 'site')
All inputs are finite; a program needn't handle non-finite values.
Results may differ from a plain program's by a relative error of at most 0.0094.
Values may be sent and summed in bfloat16 or wider, within the bound.
No kernel may reach another device: no remote copies, remote signals or barrier semaphores. Data moves between devices by JAX's collectives and lax.ppermute only.
A program may use at most 128 MiB of HBM per device.

v0:
```python
import functools

import jax
import jax.numpy as jnp
from jax import lax
from jax.experimental import pallas as pl
from jax.experimental.pallas import tpu as pltpu
from jax.sharding import PartitionSpec as P

BLK = 64
PHYS = 4
WB = 17
HALF = WB * 128
FULL = 2 * HALF
GROUPS = 8
DEPTH = 144
BF = jnp.bfloat16
F32 = jnp.float32
VMEM_BYTES = 48 * 1024 * 1024


def shape(dims, dtype=BF):
    return jax.ShapeDtypeStruct(dims, dtype)


def call(body, outs, scratch=(), smem=0, operands=(), flops=0):
    in_specs = [
        pl.BlockSpec(memory_space=pltpu.SMEM if i < smem else pltpu.VMEM)
        for i in range(len(operands))
    ]
    single = not isinstance(outs, (list, tuple))
    moved = sum(o.size * o.dtype.itemsize for o in operands)
    out_spec = pl.BlockSpec(memory_space=pltpu.VMEM)
    return pl.pallas_call(
        body,
        out_shape=outs,
        in_specs=in_specs,
        out_specs=out_spec if single else [out_spec] * len(outs),
        scratch_shapes=list(scratch),
        compiler_params=pltpu.CompilerParams(vmem_limit_bytes=VMEM_BYTES),
        cost_estimate=pl.CostEstimate(flops=flops, bytes_accessed=moved, transcendentals=0),
    )(*operands)


def iota(dims, axis):
    return lax.broadcasted_iota(jnp.int32, dims, axis)


def dot(a, b):
    return lax.dot_general(a, b, (((1,), (0,)), ((), ())), preferred_element_type=F32)


def dot_t(a, b):
    return lax.dot_general(a, b, (((1,), (1,)), ((), ())), preferred_element_type=F32)


def target(s, p):
    return (s + p % 2) % 4


def mask_body(rows_ref, cols_ref, mps_ref, all_ref, high_ref):
    row = iota((BLK, 256), 0)
    col = iota((BLK, 256), 1)
    inside = col & (BLK - 1)
    for j in range(2):
        for s in range(4):
            least = jnp.where(col < 64, cols_ref[j, s, 0], cols_ref[j, s, 1])
            most = jnp.where(col < 192, cols_ref[j, s, 2], cols_ref[j, s, 3])
            limit = jnp.where(col < 128, least, most)
            keep = jnp.logical_and(row < rows_ref[j, s], inside < limit)
            kept = jnp.where(keep, mps_ref[j, s].astype(F32), 0.0).astype(BF)
            all_ref[j, s * BLK : (s + 1) * BLK, :] = kept
            high_ref[j, s * BLK : (s + 1) * BLK, :] = kept[:, 128:]


def spread(block, step):
    tiled = jnp.concatenate([block] * 4, axis=1)
    goal = ((iota((256, 256), 0) >> 6) + step) & 3
    return jnp.where(goal == (iota((256, 256), 1) >> 6), tiled, 0.0).astype(BF)


def flipped(values, states):
    turned = values.T
    rows = []
    for t in range(4):
        parts = []
        for p in range(states):
            s = (t - p % 2) % 4
            parts.append(turned[p * BLK : (p + 1) * BLK, s * BLK : (s + 1) * BLK])
        rows.append(jnp.concatenate(parts, axis=1))
    return jnp.concatenate(rows, axis=0).astype(BF)


def enlarge(small, out_ref):
    rows = 4 * WB * 8
    up = jnp.where((iota((rows, 4 * WB), 0) >> 3) == iota((rows, 4 * WB), 1), 1.0, 0.0)
    out = jnp.where((iota((WB, DEPTH), 1) >> 3) == iota((WB, DEPTH), 0), 1.0, 0.0)
    tall = dot(up.astype(BF), small).astype(BF)
    wide = dot(tall, out.astype(BF))
    same = (iota((rows, DEPTH), 0) & 7) == (iota((rows, DEPTH), 1) & 7)
    out_ref[...] = jnp.where(same, wide, 0.0).astype(BF)


def own_ops_body(a_ref, wl_ref, wr_ref, b_ref, at_ref, kl_ref, kr_ref):
    for j in range(2):
        values = a_ref[j].astype(F32)
        for p in range(PHYS):
            b_ref[j, p] = spread(values[:, p * BLK : (p + 1) * BLK], p % 2)
        at_ref[j] = flipped(values[:, :128], 2)
    enlarge(wl_ref[...], kl_ref)
    enlarge(wr_ref[...], kr_ref)


def far_ops_body(a_ref, own_ref, b_ref, at_ref):
    for j in range(2):
        values = a_ref[j].astype(F32)
        for p in range(2):
            b_ref[j, p] = spread(values[:, p * BLK : (p + 1) * BLK], p)
        at_ref[j, :, :128] = own_ref[j]
        at_ref[j, :, 128:] = flipped(values, 2)


def raw_tile(ref, w, lt):
    cols = slice(w * BLK, (w + 1) * BLK)
    return jnp.concatenate(
        [ref[2 * lt, :, cols].astype(F32), ref[2 * lt + 1, :, cols].astype(F32)], axis=1
    )


def flat_tile(ref, w, lt):
    at = lt * HALF + w * 128
    return ref[:, at : at + 128].astype(F32)


def grouped(ref, tile, m_ref):
    for lt in range(2):
        for u in range(9):
            first = tile(ref, 2 * u, lt).reshape(GROUPS, 8, 128)
            if 2 * u + 1 < WB:
                second = tile(ref, 2 * u + 1, lt).reshape(GROUPS, 8, 128)
            else:
                second = jnp.zeros((GROUPS, 8, 128), F32)
            both = jnp.concatenate([first, second], axis=1).astype(BF)
            m_ref[:, u * 16 : (u + 1) * 16, lt * 128 : (lt + 1) * 128] = both


def mixed(m_ref, k, count, f_ref):
    for h in range(4):
        low = dot(k, m_ref[2 * h]).reshape(count * WB, 8, 256)
        high = dot(k, m_ref[2 * h + 1]).reshape(count * WB, 8, 256)
        f_ref[:, h * 16 : (h + 1) * 16, :] = jnp.concatenate([low, high], axis=1).astype(BF)


def columns(f_ref, at, b, turned, y_ref, to):
    source = f_ref[at * WB : (at + 1) * WB].reshape(WB * BLK, 256)
    out = (dot_t(source, b) if turned else dot(source, b)).astype(BF)
    for v in range(WB):
        for lt in range(2):
            y_ref[to * BLK : (to + 1) * BLK, lt * HALF + v * 128 : lt * HALF + (v + 1) * 128] = out[
                v * BLK : (v + 1) * BLK, lt * 128 : (lt + 1) * 128
            ]


def half_body(tile, turned, flat, env_ref, k_ref, b_ref, y_ref, *rest):
    if flat:
        flat_ref, m_ref, f_ref = rest
        for lt in range(2):
            for w in range(WB):
                at = lt * HALF + w * 128
                flat_ref[:, at : at + 128] = tile(env_ref, w, lt).astype(BF)
    else:
        m_ref, f_ref = rest
    grouped(env_ref, tile, m_ref)
    mixed(m_ref, k_ref[: 2 * WB * 8], 2, f_ref)
    for p in range(2):
        columns(f_ref, p, b_ref[p], turned, y_ref, p)


def own_half(env, k, b, turned, raw):
    outs = [shape((128, FULL))]
    if raw:
        outs.append(shape((BLK, FULL)))
    return call(
        functools.partial(half_body, raw_tile if raw else flat_tile, turned, raw),
        outs,
        [pltpu.VMEM((GROUPS, DEPTH, 256), BF), pltpu.VMEM((2 * WB, BLK, 256), BF)],
        operands=(env, k, b),
        flops=1_200_000_000,
    )


def full_body(tile, turned, far_at, env_ref, k_ref, b_ref, own_ref, lhs_ref, out_ref, y_ref, m_ref, f_ref):
    y_ref[:128, :] = own_ref[...]
    grouped(env_ref, tile, m_ref)
    mixed(m_ref, k_ref[2 * WB * 8 :], 2, f_ref)
    for p in range(2):
        columns(f_ref, p, b_ref[far_at + p], turned, y_ref, 2 + p)
    low = (iota((BLK, HALF), 1) & 127) < BLK
    for lt in range(2):
        both = dot(lhs_ref[lt * 128 : (lt + 1) * 128, :], y_ref[:, lt * HALF : (lt + 1) * HALF])
        out_ref[:, lt * HALF : (lt + 1) * HALF] = jnp.where(low, both[:BLK], both[BLK:]).astype(BF)


def full_update(env, k, b, own, lhs, turned, raw, far_at):
    return call(
        functools.partial(full_body, raw_tile if raw else flat_tile, turned, far_at),
        [shape((BLK, FULL)), shape((256, FULL))],
        [pltpu.VMEM((GROUPS, DEPTH, 256), BF), pltpu.VMEM((2 * WB, BLK, 256), BF)],
        operands=(env, k, b, own, lhs),
        flops=2_400_000_000,
    )


def diagonal(ref, lt, g_ref):
    lane = (iota((BLK, HALF), 1) & 127) < BLK
    low = jnp.where(lane, 1.0, 0.0).astype(BF)
    high = jnp.where(lane, 0.0, 1.0).astype(BF)
    values = ref[:, lt * HALF : (lt + 1) * HALF]
    g_ref[:BLK, :] = values * low
    g_ref[BLK:, :] = values * high


def first_body(flag_ref, got_ref, edge_ref, k_ref, b_ref, right_ref, far_ref, out_ref, m_ref, f_ref, y_ref, g_ref):
    @pl.when(flag_ref[0] == 0)
    def _():
        grouped(got_ref, flat_tile, m_ref)

    @pl.when(flag_ref[0] != 0)
    def _():
        grouped(edge_ref, flat_tile, m_ref)

    mixed(m_ref, k_ref[...], 4, f_ref)
    for p in range(PHYS):
        columns(f_ref, p, b_ref[p], False, y_ref, p)
    for lt in range(2):
        for half, source in ((0, right_ref), (1, far_ref)):
            diagonal(source, lt, g_ref)
            out_ref[half * 128 : (half + 1) * 128, lt * 128 : (lt + 1) * 128] = dot_t(
                y_ref[half * 128 : (half + 1) * 128, lt * HALF : (lt + 1) * HALF], g_ref[...]
            )


def second_body(flag_ref, got_ref, edge_ref, y_ref, first_ref, own_ref, away_ref, sums_ref, g_ref, r_ref):
    @pl.when(flag_ref[0] == 0)
    def _():
        r_ref[...] = got_ref[...]

    @pl.when(flag_ref[0] != 0)
    def _():
        r_ref[...] = edge_ref[...]

    squares = jnp.zeros((8, 128), F32)
    for lt in range(2):
        diagonal(r_ref, lt, g_ref)
        out = dot_t(y_ref[:, lt * HALF : (lt + 1) * HALF], g_ref[...])
        own_ref[:, lt * 128 : (lt + 1) * 128] = out[:128]
        away_ref[:, lt * 128 : (lt + 1) * 128] = out[128:]
        squares = squares + jnp.sum((out * out).reshape(32, 8, 128), axis=0)
    first = first_ref[...]
    sums = jnp.sum((first * first).reshape(32, 8, 256), axis=0)
    total_first = jnp.sum(sums)
    total_second = jnp.sum(squares)
    both = jnp.where(iota((16, 8, 128), 1) < 4, total_first, total_second)
    sums_ref[...] = both


def final_body(entries, first_ref, own_ref, away_ref, sums_ref, out_ref):
    total = jnp.sum(sums_ref[...], axis=0)
    scale = lax.rsqrt(total * (1.0 / entries) + 1e-06)
    for j in range(2):
        factor = scale[4 * j : 4 * j + 1, :1]
        for s in range(4):
            parts = []
            for p in range(PHYS):
                t = target(s, p)
                if j == 0:
                    ref, at = first_ref, p * BLK
                elif p < 2:
                    ref, at = own_ref, p * BLK
                else:
                    ref, at = away_ref, (p - 2) * BLK
                parts.append(ref[at : at + BLK, t * BLK : (t + 1) * BLK])
            out_ref[j, s] = jnp.concatenate(parts, axis=1) * factor


def passed_along(block, axis, distance):
    devices = lax.axis_size(axis)
    route = [(i, (i + distance) % devices) for i in range(devices)]
    return lax.ppermute(block, axis, route)


def shifted(value, axis, by):
    devices = lax.axis_size(axis)
    pairs = [(i, i + by) for i in range(devices) if 0 <= i + by < devices]
    return lax.ppermute(value, axis, pairs)


def local(mps, left_env, right_env, row_fill, col_fill, mpo_values, mpo_pattern):
    left_raw, right_raw = left_env[0], right_env[0]
    left_behind = passed_along(left_raw, "site", 1)
    right_ahead = passed_along(right_raw, "site", -1)
    weights = mpo_values * mpo_pattern.astype(BF)
    left_small = weights.transpose(2, 1, 0).reshape(PHYS * WB, WB)
    right_small = weights.transpose(2, 0, 1).reshape(PHYS * WB, WB)
    masked, high = call(
        mask_body,
        [shape((2, 256, 256)), shape((2, 256, 128))],
        smem=2,
        operands=(row_fill, col_fill, mps),
    )
    high_behind = passed_along(high, "site", 1)
    blocks, turned_own, k_left, k_right = call(
        own_ops_body,
        [
            shape((2, PHYS, 256, 256)),
            shape((2, 256, 128)),
            shape((4 * WB * 8, DEPTH)),
            shape((4 * WB * 8, DEPTH)),
        ],
        operands=(masked, left_small, right_small),
        flops=100_000_000,
    )
    far_blocks, turned = call(
        far_ops_body,
        [shape((2, 2, 256, 256)), shape((2, 256, 256))],
        operands=(high_behind, turned_own),
    )
    left_part, left_edge = own_half(left_raw, k_left, blocks[0], False, True)
    right_part, right_edge = own_half(right_raw, k_right, blocks[1], True, True)
    left_one, _ = full_update(
        left_behind, k_left, far_blocks[0], left_part, turned[0], False, True, 0
    )
    left_one_behind = passed_along(left_one, "site", 1)
    right_one, _ = full_update(
        right_ahead, k_right, blocks[1], right_part, masked[1], True, True, 2
    )
    right_one_ahead = passed_along(right_one, "site", -1)
    (left_part,) = own_half(left_one, k_left, blocks[1], False, False)
    (right_part,) = own_half(right_one, k_right, blocks[0], True, False)
    left_out, second_mixed = full_update(
        left_one_behind, k_left, far_blocks[1], left_part, turned[1], False, False, 0
    )
    left_got = shifted(left_out, "sector", 1)
    right_out, _ = full_update(
        right_one_ahead, k_right, blocks[0], right_part, masked[0], True, False, 2
    )
    right_got = shifted(right_out, "sector", -1)
    position = lax.axis_index("sector")
    first_flag = (position == 0).astype(jnp.int32).reshape(1)
    last_flag = (position == lax.axis_size("sector") - 1).astype(jnp.int32).reshape(1)
    first = call(
        first_body,
        shape((256, 256), F32),
        [
            pltpu.VMEM((GROUPS, DEPTH, 256), BF),
            pltpu.VMEM((4 * WB, BLK, 256), BF),
            pltpu.VMEM((256, FULL), BF),
            pltpu.VMEM((128, HALF), BF),
        ],
        smem=1,
        operands=(first_flag, left_got, left_edge, k_left, blocks[0], right_one, right_one_ahead),
        flops=3_000_000_000,
    )
    own, away, sums = call(
        second_body,
        [shape((128, 256), F32), shape((128, 256), F32), shape((16, 8, 128), F32)],
        [pltpu.VMEM((128, HALF), BF), pltpu.VMEM((BLK, FULL), BF)],
        smem=1,
        operands=(last_flag, right_got, right_edge, second_mixed, first),
        flops=1_000_000_000,
    )
    devices = lax.axis_size("site")
    gathered = lax.all_to_all(sums[:devices], "site", 0, 0, tiled=True)
    back = passed_along(away, "site", -1)
    return call(
        functools.partial(final_body, 256 * 256 * devices),
        shape((2, 4, BLK, 256), F32),
        operands=(first, own, back, gathered),
    )


def solution(mesh):
    in_specs = (
        P("sector", "site", None, None),
        P("sector", "site", None, None),
        P("sector", "site", None, None),
        P("sector", "site"),
        P("sector", "site", None),
        P(),
        P(),
    )
    out_specs = P("sector", "site", None, None)
    return jax.shard_map(local, mesh=mesh, in_specs=in_specs, out_specs=out_specs, check_vma=False)
```

profile of v0, /device:TPU:199, one launch (start us, length us, event | category | flops | bytes accessed | tf_op | source)
XLA Modules:
  0.0 74.8 jit_solution(3969810338447132944)
XLA Ops:
  0.0 0.7 collective-permute-start.4
  0.7 0.0 copy-start
  0.7 0.9 %copy-done = bf16[2,4,64,256]{3,2,1,0:T(8,128)(2,1)S(1)} copy-done((bf16[2,4,64,256]{3,2,1,0:T(8,128)(2,1)S(1)}, bf16[2,4,64,256]{3,2,1,0:T(8,128)(2,1)}, u32[]{:S(2)}) %copy-start) | copy-done | bytes 262168
  1.6 0.0 copy-start.1
  1.6 0.7 copy-done.1
  2.3 0.0 copy-start.2
  2.3 0.7 copy-done.2
  3.0 0.0 copy-start.3
  3.0 0.7 shard_map.73
  3.7 1.2 %collective-permute-start.1 = (bf16[2,256,128]{2,1,0:T(8,128)(2,1)S(1)}, bf16[2,256,128]{2,1,0:T(8,128)(2,1)S(1)}, u32[]{:S(2)}, u32[]{:S(2)}) collective-permute-start(bf16[2,256,128]{2,1,0:T(8,128)(2,1)S(1)} %get-tuple-element.27), channel_id=1, source_target_pairs={{0,32},{32,64},{64,96},{96,128},{128,160},{160,192},{192,224},{224... | collective-permute-start | bytes 393224 | tf_op jit(solution)/shard_map/ppermute | solution.py:289
  4.9 0.5 collective-permute-start
  5.4 0.8 %fusion = (bf16[4,17,17]{2,0,1:T(4,128)(2,1)S(1)}, bf16[4,17,17]{1,0,2:T(4,128)(2,1)S(1)}) fusion(bf16[17,17,4]{1,2,0:T(4,128)(2,1)} %param.12, s32[17,17,4]{1,2,0:T(4,128)} %param.13), kind=kLoop, calls=%fused_computation.9 | loop fusion | flops 2312 | bytes 11560 | tf_op jit(solution)/shard_map/transpose | solution.py:304
  6.2 0.1 reshape.18
  6.3 0.1 copy.11.wl_ref
  6.5 0.8 %shard_map.74 = (bf16[2,4,256,256]{3,2,1,0:T(8,128)(2,1)S(1)}, bf16[2,256,128]{2,1,0:T(8,128)(2,1)S(1)}, bf16[544,144]{1,0:T(8,128)(2,1)S(1)}, bf16[544,144]{1,0:T(8,128)(2,1)S(1)}) custom-call(bf16[2,256,256]{2,1,0:T(8,128)(2,1)S(1)} %get-tuple-element.25.a_ref, bf16[68,17]{1,0:T(8,128)(2,1)S(1)} %copy.11.wl_ref, bf16[68,17]{1,0:T(8,128)(2,1)S(1)} %reshape.26.wr_ref), custom_call_target="tpu_custom_call" | custom-call | flops 100000000 | bytes 266768 | tf_op jit(solution)/shard_map/pallas_call | solution.py:34
  7.2 0.0 copy-start.9
  7.2 0.1 slice_bitcast_fusion
  7.3 0.0 copy-done.3
  7.4 1.0 %shard_map.76 = (bf16[128,4352]{1,0:T(8,128)(2,1)S(1)}, bf16[64,4352]{1,0:T(8,128)(2,1)S(1)}) custom-call(bf16[4,64,1088]{2,1,0:T(8,128)(2,1)S(1)} %bitcast.27, bf16[544,144]{1,0:T(8,128)(2,1)S(1)} %get-tuple-element.26.k_ref, bf16[4,256,256]{2,1,0:T(8,128)(2,1)S(1)} %get-tuple-element.46.b_ref), custom_call_target="tpu_custom_call" | custom-call | flops 1200000000 | bytes 1238016 | tf_op jit(solution)/shard_map/pallas_call | solution.py:34
  8.3 0.0 copy-start.11
  8.3 0.0 collective-permute-done.1.a_ref
  8.4 0.4 shard_map.75
  8.8 0.4 copy-done.11
  9.2 4.1 %collective-permute-done.env_ref = bf16[4,64,1088]{2,1,0:T(8,128)(2,1)S(1)} collective-permute-done((bf16[4,64,1088]{2,1,0:T(8,128)(2,1)}, bf16[4,64,1088]{2,1,0:T(8,128)(2,1)S(1)}, u32[]{:S(2)}, u32[]{:S(2)}) %collective-permute-start) | collective-permute-done | bytes 557088 | tf_op jit(solution)/shard_map/ppermute | solution.py:289
  13.2 0.0 copy-start.4
  13.2 2.5 %shard_map.77 = (bf16[64,4352]{1,0:T(8,128)(2,1)S(1)}, bf16[256,4352]{1,0:T(8,128)(2,1)}) custom-call(bf16[4,64,1088]{2,1,0:T(8,128)(2,1)S(1)} %collective-permute-done.env_ref, bf16[544,144]{1,0:T(8,128)(2,1)S(1)} %get-tuple-element.26.k_ref, bf16[2,256,256]{2,1,0:T(8,128)(2,1)S(1)} %get-tuple-element.48.b_ref, ...), custom_call_target="tpu_custom_call" | custom-call | flops 2400000000 | bytes 2221056 | tf_op jit(solution)/shard_map/pallas_call | solution.py:34
  15.7 2.4 %collective-permute-start.2 = (bf16[64,4352]{1,0:T(8,128)(2,1)S(1)}, bf16[64,4352]{1,0:T(8,128)(2,1)S(1)}, u32[]{:S(2)}, u32[]{:S(2)}) collective-permute-start(bf16[64,4352]{1,0:T(8,128)(2,1)S(1)} %get-tuple-element.33.env_ref), channel_id=1, source_target_pairs={{0,32},{32,64},{64,96},{96,128},{128,160},{160,192},{192,224},{224... | collective-permute-start | bytes 1671176 | tf_op jit(solution)/shard_map/ppermute | solution.py:289
  18.1 0.0 copy-done.4
  18.1 1.0 %shard_map.80 = (bf16[128,4352]{1,0:T(8,128)(2,1)S(1)}, bf16[64,4352]{1,0:T(8,128)(2,1)S(1)}) custom-call(bf16[4,64,1088]{2,1,0:T(8,128)(2,1)S(1)} %bitcast.29, bf16[544,144]{1,0:T(8,128)(2,1)S(1)} %get-tuple-element.36.k_ref, bf16[4,256,256]{2,1,0:T(8,128)(2,1)S(1)} %get-tuple-element.45.b_ref), custom_call_target="tpu_custom_call" | custom-call | flops 1200000000 | bytes 1238016 | tf_op jit(solution)/shard_map/pallas_call | solution.py:34
  19.0 0.0 copy-start.7
  19.0 0.8 %copy-done.7 = bf16[64,4352]{1,0:T(8,128)(2,1)} copy-done((bf16[64,4352]{1,0:T(8,128)(2,1)}, bf16[64,4352]{1,0:T(8,128)(2,1)S(1)}, u32[]{:S(2)}) %copy-start.7) | copy-done | bytes 557080
  19.8 0.0 collective-permute-done.4.env_ref
  19.8 2.5 %shard_map.81 = (bf16[64,4352]{1,0:T(8,128)(2,1)S(1)}, bf16[256,4352]{1,0:T(8,128)(2,1)}) custom-call(bf16[4,64,1088]{2,1,0:T(8,128)(2,1)S(1)} %collective-permute-done.4.env_ref, bf16[544,144]{1,0:T(8,128)(2,1)S(1)} %get-tuple-element.36.k_ref, bf16[4,256,256]{2,1,0:T(8,128)(2,1)S(1)} %get-tuple-element.45.b_ref, ...), custom_call_target="tpu_custom_call" | custom-call | flops 2400000000 | bytes 2483200 | tf_op jit(solution)/shard_map/pallas_call | solution.py:34
  22.3 2.9 %collective-permute-start.5 = (bf16[64,4352]{1,0:T(8,128)(2,1)S(1)}, bf16[64,4352]{1,0:T(8,128)(2,1)S(1)}, u32[]{:S(2)}, u32[]{:S(2)}) collective-permute-start(bf16[64,4352]{1,0:T(8,128)(2,1)S(1)} %get-tuple-element.38.right_ref.env_ref), channel_id=1, source_target_pairs={{0,480},{32,0},{64,32},{96,64},{128,96},{160,128},{192,160},{224,1... | collective-permute-start | bytes 1671176 | tf_op jit(solution)/shard_map/ppermute | solution.py:289
  25.2 0.9 %shard_map.78.own_ref = bf16[128,4352]{1,0:T(8,128)(2,1)S(1)} custom-call(bf16[64,4352]{1,0:T(8,128)(2,1)S(1)} %get-tuple-element.33.env_ref, bf16[544,144]{1,0:T(8,128)(2,1)S(1)} %get-tuple-element.26.k_ref, bf16[4,256,256]{2,1,0:T(8,128)(2,1)S(1)} %get-tuple-element.45.b_ref), custom_call_target="tpu_custom_call" | custom-call | flops 1200000000 | bytes 1238016 | tf_op jit(solution)/shard_map/pallas_call | solution.py:34
  26.1 0.0 collective-permute-done.2.env_ref
  26.1 0.0 copy-done.9
  26.1 1.2 %shard_map.79 = (bf16[64,4352]{1,0:T(8,128)(2,1)S(1)}, bf16[256,4352]{1,0:T(8,128)(2,1)S(1)}) custom-call(bf16[64,4352]{1,0:T(8,128)(2,1)S(1)} %collective-permute-done.2.env_ref, bf16[544,144]{1,0:T(8,128)(2,1)S(1)} %get-tuple-element.26.k_ref, bf16[2,256,256]{2,1,0:T(8,128)(2,1)S(1)} %get-tuple-element.47.b_ref, bf16[128,4352]{1,0:T(8,128)(2,1)S(1)} %shard_map.78.own_ref, ...), custom_call_target="tpu_custom_call" | custom-call | flops 2400000000 | bytes 2221056 | tf_op jit(solution)/shard_map/pallas_call | solution.py:34
  27.3 0.0 copy-start.5
  27.3 1.4 %copy-done.5 = bf16[256,4352]{1,0:T(8,128)(2,1)} copy-done((bf16[256,4352]{1,0:T(8,128)(2,1)}, bf16[256,4352]{1,0:T(8,128)(2,1)S(1)}, u32[]{:S(2)}) %copy-start.5) | copy-done | bytes 2228248
  28.7 5.1 %collective-permute-start.3 = (bf16[64,4352]{1,0:T(8,128)(2,1)S(1)}, bf16[64,4352]{1,0:T(8,128)(2,1)S(1)}, u32[]{:S(2)}, u32[]{:S(2)}) collective-permute-start(bf16[64,4352]{1,0:T(8,128)(2,1)S(1)} %get-tuple-element.34), channel_id=1, source_target_pairs={{0,1},{1,2},{2,3},{3,4},{4,5},{5,6},{6,7},{7,8},{8,9},{9,10},{10,1... | collective-permute-start | bytes 1671176 | tf_op jit(solution)/shard_map/ppermute | solution.py:295
  33.9 0.9 %shard_map.83.own_ref = bf16[128,4352]{1,0:T(8,128)(2,1)S(1)} custom-call(bf16[64,4352]{1,0:T(8,128)(2,1)S(1)} %get-tuple-element.38.right_ref.env_ref, bf16[544,144]{1,0:T(8,128)(2,1)S(1)} %get-tuple-element.36.k_ref, bf16[4,256,256]{2,1,0:T(8,128)(2,1)S(1)} %get-tuple-element.46.b_ref), custom_call_target="tpu_custom_call" | custom-call | flops 1200000000 | bytes 1238016 | tf_op jit(solution)/shard_map/pallas_call | solution.py:34
  34.7 0.0 collective-permute-done.5.far_ref.env_ref
  34.7 2.6 %shard_map.84 = (bf16[64,4352]{1,0:T(8,128)(2,1)}, bf16[256,4352]{1,0:T(8,128)(2,1)}) custom-call(bf16[64,4352]{1,0:T(8,128)(2,1)S(1)} %collective-permute-done.5.far_ref.env_ref, bf16[544,144]{1,0:T(8,128)(2,1)S(1)} %get-tuple-element.36.k_ref, bf16[4,256,256]{2,1,0:T(8,128)(2,1)S(1)} %get-tuple-element.46.b_ref, bf16[128,4352]{1,0:T(8,128)(2,1)S(1)} %shard_map.83.own_ref, ...), custom_call_target="tpu_custom_call" | custom-call | flops 2400000000 | bytes 2483200 | tf_op jit(solution)/shard_map/pallas_call | solution.py:34
  37.3 1.9 %collective-permute-start.6 = (bf16[64,4352]{1,0:T(8,128)(2,1)}, bf16[64,4352]{1,0:T(8,128)(2,1)S(1)}, u32[]{:S(2)}, u32[]{:S(2)}) collective-permute-start(bf16[64,4352]{1,0:T(8,128)(2,1)} %get-tuple-element.39), channel_id=1, source_target_pairs={{1,0},{2,1},{3,2},{4,3},{5,4},{6,5},{7,6},{8,7},{9,8},{10,9},{11,1... | collective-permute-start | bytes 1671176 | tf_op jit(solution)/shard_map/ppermute | solution.py:295
  39.3 1.4 %collective-permute-done.3.got_ref = bf16[64,4352]{1,0:T(8,128)(2,1)S(1)} collective-permute-done((bf16[64,4352]{1,0:T(8,128)(2,1)S(1)}, bf16[64,4352]{1,0:T(8,128)(2,1)S(1)}, u32[]{:S(2)}, u32[]{:S(2)}) %collective-permute-start.3) | collective-permute-done | bytes 557088 | tf_op jit(solution)/shard_map/ppermute | solution.py:295
  40.7 0.0 copy-start.10
  40.7 1.0 %copy-done.10 = bf16[544,144]{1,0:T(8,128)(2,1)S(1)} copy-done((bf16[544,144]{1,0:T(8,128)(2,1)S(1)}, bf16[544,144]{1,0:T(8,128)(2,1)}, u32[]{:S(2)}) %copy-start.10) | copy-done | bytes 156696
  41.7 0.0 copy-start.12
  41.7 1.1 %copy-done.12 = bf16[64,4352]{1,0:T(8,128)(2,1)S(1)} copy-done((bf16[64,4352]{1,0:T(8,128)(2,1)S(1)}, bf16[64,4352]{1,0:T(8,128)(2,1)}, u32[]{:S(2)}) %copy-start.12) | copy-done | bytes 557080
  42.7 0.0 copy-start.6
  42.7 0.0 copy-start.8
  42.7 2.2 %shard_map.82.first_ref = f32[256,256]{1,0:T(8,128)S(1)} custom-call(s32[1]{0:T(128)} %bitcast.flag_ref, bf16[64,4352]{1,0:T(8,128)(2,1)S(1)} %collective-permute-done.3.got_ref, bf16[64,4352]{1,0:T(8,128)(2,1)S(1)} %copy-done.12, bf16[544,144]{1,0:T(8,128)(2,1)S(1)} %copy-done.10, bf16[4,256,256]{2,1,0:T(8,128)(2,1)S(1)} %get-tuple-element.46.b_ref, ...), custom_call_target="tpu_custom_call" | custom-call | flops 3000000000 | bytes 2909188 | tf_op jit(solution)/shard_map/pallas_call | solution.py:34
  44.9 6.6 %collective-permute-done.6.got_ref = bf16[64,4352]{1,0:T(8,128)(2,1)S(1)} collective-permute-done((bf16[64,4352]{1,0:T(8,128)(2,1)}, bf16[64,4352]{1,0:T(8,128)(2,1)S(1)}, u32[]{:S(2)}, u32[]{:S(2)}) %collective-permute-start.6) | collective-permute-done | bytes 557088 | tf_op jit(solution)/shard_map/ppermute | solution.py:295
  51.5 0.0 copy-done.6
  51.5 0.0 copy-done.8
  51.5 0.9 %shard_map.85 = (f32[128,256]{1,0:T(8,128)S(1)}, f32[128,256]{1,0:T(8,128)S(1)}, f32[16,8,128]{2,1,0:T(8,128)S(1)}) custom-call(s32[1]{0:T(128)} %bitcast.12.flag_ref, bf16[64,4352]{1,0:T(8,128)(2,1)S(1)} %collective-permute-done.6.got_ref, bf16[64,4352]{1,0:T(8,128)(2,1)S(1)} %copy-done.8, bf16[256,4352]{1,0:T(8,128)(2,1)S(1)} %copy-done.6, ...), custom_call_target="tpu_custom_call" | custom-call | flops 1000000000 | bytes 3604484 | tf_op jit(solution)/shard_map/pallas_call | solution.py:34
  52.5 6.3 %collective-permute-start.7 = (f32[128,256]{1,0:T(8,128)S(1)}, f32[128,256]{1,0:T(8,128)S(1)}, u32[]{:S(2)}, u32[]{:S(2)}) collective-permute-start(f32[128,256]{1,0:T(8,128)S(1)} %get-tuple-element.43), channel_id=1, source_target_pairs={{0,480},{32,0},{64,32},{96,64},{128,96},{160,128},{192,160},{224,1... | collective-permute-start | bytes 393224 | tf_op jit(solution)/shard_map/ppermute | solution.py:289
  58.7 15.0 %all_to_all.5.sums_ref = f32[16,8,128]{2,1,0:T(8,128)S(1)} all-to-all(f32[16,8,128]{2,1,0:T(8,128)S(1)} %get-tuple-element.44), channel_id=1, replica_groups=mesh['site'=16,'sector'=32] {'site'}, dimensions={0} | all-to-all | bytes 131072 | tf_op jit(solution)/shard_map/all_to_all | solution.py:373
  73.8 0.0 collective-permute-done.7.away_ref
  73.8 1.0 %shard_map.86 = f32[2,4,64,256]{3,2,1,0:T(8,128)} custom-call(f32[256,256]{1,0:T(8,128)S(1)} %shard_map.82.first_ref, f32[128,256]{1,0:T(8,128)S(1)} %get-tuple-element.42.own_ref, f32[128,256]{1,0:T(8,128)S(1)} %collective-permute-done.7.away_ref, f32[16,8,128]{2,1,0:T(8,128)S(1)} %all_to_all.5.sums_ref), custom_call_target="tpu_custom_call" | custom-call | bytes 589824 | tf_op jit(solution)/shard_map/pallas_call | solution.py:34
  (5 shorter events, 0.1 us)
Async XLA Ops:
  0.0 19.8 %collective-permute-start.4 = (bf16[4,64,1088]{2,1,0:T(8,128)(2,1)}, bf16[4,64,1088]{2,1,0:T(8,128)(2,1)S(1)}, u32[]{:S(2)}, u32[]{:S(2)}) collective-permute-start(bf16[4,64,1088]{2,1,0:T(8,128)(2,1)} %bitcast.28), channel_id=1, source_target_pairs={{0,480},{32,0},{64,32},{96,64},{128,96},{160,128},{192,160},{224,1... | collective-permute-start | bytes 1671176 | tf_op jit(solution)/shard_map/ppermute | solution.py:289
  0.7 0.9 %copy-start = (bf16[2,4,64,256]{3,2,1,0:T(8,128)(2,1)S(1)}, bf16[2,4,64,256]{3,2,1,0:T(8,128)(2,1)}, u32[]{:S(2)}) copy-start(bf16[2,4,64,256]{3,2,1,0:T(8,128)(2,1)} %mps_ref.1) | copy-start | bytes 786436
  1.6 0.7 copy-start.1
  2.3 0.7 copy-start.2
  3.0 4.3 %copy-start.3 = (bf16[1,4,64,1088]{3,2,1,0:T(8,128)(2,1)S(1)}, bf16[1,4,64,1088]{3,2,1,0:T(8,128)(2,1)}, u32[]{:S(2)}) copy-start(bf16[1,4,64,1088]{3,2,1,0:T(8,128)(2,1)} %param.8) | copy-start | bytes 1671172
  3.7 4.6 %collective-permute-start.1 = (bf16[2,256,128]{2,1,0:T(8,128)(2,1)S(1)}, bf16[2,256,128]{2,1,0:T(8,128)(2,1)S(1)}, u32[]{:S(2)}, u32[]{:S(2)}) collective-permute-start(bf16[2,256,128]{2,1,0:T(8,128)(2,1)S(1)} %get-tuple-element.27), channel_id=1, source_target_pairs={{0,32},{32,64},{64,96},{96,128},{128,160},{160,192},{192,224},{224... | collective-permute-start | bytes 393224 | tf_op jit(solution)/shard_map/ppermute | solution.py:289
  4.9 8.3 %collective-permute-start = (bf16[4,64,1088]{2,1,0:T(8,128)(2,1)}, bf16[4,64,1088]{2,1,0:T(8,128)(2,1)S(1)}, u32[]{:S(2)}, u32[]{:S(2)}) collective-permute-start(bf16[4,64,1088]{2,1,0:T(8,128)(2,1)} %bitcast.26), channel_id=1, source_target_pairs={{0,32},{32,64},{64,96},{96,128},{128,160},{160,192},{192,224},{224... | collective-permute-start | bytes 1671176 | tf_op jit(solution)/shard_map/ppermute | solution.py:289
  7.2 18.9 %copy-start.9 = (bf16[544,144]{1,0:T(8,128)(2,1)}, bf16[544,144]{1,0:T(8,128)(2,1)S(1)}, u32[]{:S(2)}) copy-start(bf16[544,144]{1,0:T(8,128)(2,1)S(1)} %get-tuple-element.26.k_ref) | copy-start | bytes 470020
  8.3 0.8 %copy-start.11 = (bf16[64,4352]{1,0:T(8,128)(2,1)}, bf16[64,4352]{1,0:T(8,128)(2,1)S(1)}, u32[]{:S(2)}) copy-start(bf16[64,4352]{1,0:T(8,128)(2,1)S(1)} %get-tuple-element.35.edge_ref) | copy-start | bytes 1671172
  13.2 4.8 %copy-start.4 = (bf16[1,4,64,1088]{3,2,1,0:T(8,128)(2,1)S(1)}, bf16[1,4,64,1088]{3,2,1,0:T(8,128)(2,1)}, u32[]{:S(2)}) copy-start(bf16[1,4,64,1088]{3,2,1,0:T(8,128)(2,1)} %param.9) | copy-start | bytes 1671172
  15.7 10.4 %collective-permute-start.2 = (bf16[64,4352]{1,0:T(8,128)(2,1)S(1)}, bf16[64,4352]{1,0:T(8,128)(2,1)S(1)}, u32[]{:S(2)}, u32[]{:S(2)}) collective-permute-start(bf16[64,4352]{1,0:T(8,128)(2,1)S(1)} %get-tuple-element.33.env_ref), channel_id=1, source_target_pairs={{0,32},{32,64},{64,96},{96,128},{128,160},{160,192},{192,224},{224... | collective-permute-start | bytes 1671176 | tf_op jit(solution)/shard_map/ppermute | solution.py:289
  19.0 0.8 %copy-start.7 = (bf16[64,4352]{1,0:T(8,128)(2,1)}, bf16[64,4352]{1,0:T(8,128)(2,1)S(1)}, u32[]{:S(2)}) copy-start(bf16[64,4352]{1,0:T(8,128)(2,1)S(1)} %get-tuple-element.40.edge_ref) | copy-start | bytes 1671172
  22.3 12.4 %collective-permute-start.5 = (bf16[64,4352]{1,0:T(8,128)(2,1)S(1)}, bf16[64,4352]{1,0:T(8,128)(2,1)S(1)}, u32[]{:S(2)}, u32[]{:S(2)}) collective-permute-start(bf16[64,4352]{1,0:T(8,128)(2,1)S(1)} %get-tuple-element.38.right_ref.env_ref), channel_id=1, source_target_pairs={{0,480},{32,0},{64,32},{96,64},{128,96},{160,128},{192,160},{224,1... | collective-permute-start | bytes 1671176 | tf_op jit(solution)/shard_map/ppermute | solution.py:289
  27.3 1.4 %copy-start.5 = (bf16[256,4352]{1,0:T(8,128)(2,1)}, bf16[256,4352]{1,0:T(8,128)(2,1)S(1)}, u32[]{:S(2)}) copy-start(bf16[256,4352]{1,0:T(8,128)(2,1)S(1)} %get-tuple-element.41.y_ref) | copy-start | bytes 6684676
  28.7 12.0 %collective-permute-start.3 = (bf16[64,4352]{1,0:T(8,128)(2,1)S(1)}, bf16[64,4352]{1,0:T(8,128)(2,1)S(1)}, u32[]{:S(2)}, u32[]{:S(2)}) collective-permute-start(bf16[64,4352]{1,0:T(8,128)(2,1)S(1)} %get-tuple-element.34), channel_id=1, source_target_pairs={{0,1},{1,2},{2,3},{3,4},{4,5},{5,6},{6,7},{7,8},{8,9},{9,10},{10,1... | collective-permute-start | bytes 1671176 | tf_op jit(solution)/shard_map/ppermute | solution.py:295
  37.3 14.2 %collective-permute-start.6 = (bf16[64,4352]{1,0:T(8,128)(2,1)}, bf16[64,4352]{1,0:T(8,128)(2,1)S(1)}, u32[]{:S(2)}, u32[]{:S(2)}) collective-permute-start(bf16[64,4352]{1,0:T(8,128)(2,1)} %get-tuple-element.39), channel_id=1, source_target_pairs={{1,0},{2,1},{3,2},{4,3},{5,4},{6,5},{7,6},{8,7},{9,8},{10,9},{11,1... | collective-permute-start | bytes 1671176 | tf_op jit(solution)/shard_map/ppermute | solution.py:295
  40.7 1.0 %copy-start.10 = (bf16[544,144]{1,0:T(8,128)(2,1)S(1)}, bf16[544,144]{1,0:T(8,128)(2,1)}, u32[]{:S(2)}) copy-start(bf16[544,144]{1,0:T(8,128)(2,1)} %copy-done.9) | copy-start | bytes 470020
  41.7 1.1 %copy-start.12 = (bf16[64,4352]{1,0:T(8,128)(2,1)S(1)}, bf16[64,4352]{1,0:T(8,128)(2,1)}, u32[]{:S(2)}) copy-start(bf16[64,4352]{1,0:T(8,128)(2,1)} %copy-done.11) | copy-start | bytes 1671172
  42.7 8.8 %copy-start.6 = (bf16[256,4352]{1,0:T(8,128)(2,1)S(1)}, bf16[256,4352]{1,0:T(8,128)(2,1)}, u32[]{:S(2)}) copy-start(bf16[256,4352]{1,0:T(8,128)(2,1)} %copy-done.5) | copy-start | bytes 6684676
  42.7 8.8 %copy-start.8 = (bf16[64,4352]{1,0:T(8,128)(2,1)S(1)}, bf16[64,4352]{1,0:T(8,128)(2,1)}, u32[]{:S(2)}) copy-start(bf16[64,4352]{1,0:T(8,128)(2,1)} %copy-done.7) | copy-start | bytes 1671172
  52.5 21.3 %collective-permute-start.7 = (f32[128,256]{1,0:T(8,128)S(1)}, f32[128,256]{1,0:T(8,128)S(1)}, u32[]{:S(2)}, u32[]{:S(2)}) collective-permute-start(f32[128,256]{1,0:T(8,128)S(1)} %get-tuple-element.43), channel_id=1, source_target_pairs={{0,480},{32,0},{64,32},{96,64},{128,96},{160,128},{192,160},{224,1... | collective-permute-start | bytes 393224 | tf_op jit(solution)/shard_map/ppermute | solution.py:289
where the time goes:
time: 75.2 us; the launch traced here: 74.8 us
  starting transfers between devices  21 us (28%)
  Pallas kernels  18.3 us (24%)
  blocking collectives  15 us (20%)
  waiting for transfers between devices  12.1 us (16%)
  local copies, waits for them, and re-layouts  7.3 us (10%)
  other arithmetic  0.79 us (1%)
    pallas_call x14, Pallas kernels, call(): pl.pallas_call(body, out_shape=outs, in_specs=in_specs, out_specs=out_spe...  18.3 us
    all_to_all x1, blocking collectives, local(): gathered = lax.all_to_all(sums[:devices], 'site', 0, 0, tiled=True)  15 us
    ppermute x6, starting transfers between devices, passed_along(): return lax.ppermute(block, axis, route)  14 us
    ppermute x2, waiting for transfers between devices, shifted(): return lax.ppermute(value, axis, pairs)  8.04 us
    ppermute x2, starting transfers between devices, shifted(): return lax.ppermute(value, axis, pairs)  7.02 us
    unnamed x26, local copies, waits for them, and re-layouts  6.91 us
    ppermute x6, waiting for transfers between devices, passed_along(): return lax.ppermute(block, axis, route)  4.08 us
  transfers between devices with their start and end apart: 8, of which 3 were waited for; matrix products, arithmetic and copies ran while one was open for 2% of the time, Pallas kernels for 22%

commit v1 on v0

v1 whole, which is shorter than its diff:
```python
import functools

import jax
import jax.numpy as jnp
from jax import lax
from jax.experimental import pallas as pl
from jax.experimental.pallas import tpu as pltpu
from jax.sharding import PartitionSpec as P

BLK = 64
PHYS = 4
WB = 17
HALF = WB * 128
FULL = 2 * HALF
GROUPS = 8
DEPTH = 144
BF = jnp.bfloat16
F32 = jnp.float32


def shape(dims, dtype=BF):
    return jax.ShapeDtypeStruct(dims, dtype)


def call(body, outs, scratch=(), smem=0, hbm=0, operands=(), after=(), mib=16, us=1.20):
    spaces = [pltpu.SMEM] * smem + [pltpu.HBM] * hbm
    spaces += [pltpu.VMEM] * (len(operands) - len(spaces))
    spaces += [pl.ANY] * len(after)
    single = not isinstance(outs, (list, tuple))
    out_spec = pl.BlockSpec(memory_space=pltpu.VMEM)
    count = len(operands)

    def ordered(*refs):
        body(*refs[:count], *refs[count + len(after) :])

    return pl.pallas_call(
        ordered,
        out_shape=outs,
        in_specs=[pl.BlockSpec(memory_space=space) for space in spaces],
        out_specs=out_spec if single else [out_spec] * len(outs),
        scratch_shapes=list(scratch),
        compiler_params=pltpu.CompilerParams(vmem_limit_bytes=mib * 1024 * 1024),
        cost_estimate=pl.CostEstimate(flops=int(us * 1.1e9), bytes_accessed=1, transcendentals=0),
    )(*operands, *after)


def iota(dims, axis):
    return lax.broadcasted_iota(jnp.int32, dims, axis)


def dot(a, b):
    return lax.dot_general(a, b, (((1,), (0,)), ((), ())), preferred_element_type=F32)


def dot_t(a, b):
    return lax.dot_general(a, b, (((1,), (1,)), ((), ())), preferred_element_type=F32)


def target(s, p):
    return (s + p % 2) % 4


def keep_inside(rows_hbm, cols_hbm, mps_hbm, all_ref, high_ref, rows_ref, cols_ref, mps_ref, sems):
    pairs = ((rows_hbm, rows_ref), (cols_hbm, cols_ref), (mps_hbm, mps_ref))
    copies = [pltpu.make_async_copy(a, b, sems.at[i]) for i, (a, b) in enumerate(pairs)]
    for copy in copies:
        copy.start()
    for copy in copies:
        copy.wait()
    row = iota((BLK, 256), 0)
    col = iota((BLK, 256), 1)
    inside = col & (BLK - 1)
    for j in range(2):
        for s in range(4):
            least = jnp.where(col < 64, cols_ref[j, s, 0], cols_ref[j, s, 1])
            most = jnp.where(col < 192, cols_ref[j, s, 2], cols_ref[j, s, 3])
            limit = jnp.where(col < 128, least, most)
            keep = jnp.logical_and(row < rows_ref[j, s], inside < limit)
            kept = jnp.where(keep, mps_ref[j, s].astype(F32), 0.0).astype(BF)
            all_ref[j, s * BLK : (s + 1) * BLK, :] = kept
            high_ref[j, s * BLK : (s + 1) * BLK, :] = kept[:, 128:]


def spread(block, step):
    tiled = jnp.concatenate([block] * 4, axis=1)
    goal = ((iota((256, 256), 0) >> 6) + step) & 3
    return jnp.where(goal == (iota((256, 256), 1) >> 6), tiled, 0.0).astype(BF)


def flipped(values, states):
    turned = values.T
    rows = []
    for t in range(4):
        parts = []
        for p in range(states):
            s = (t - p % 2) % 4
            parts.append(turned[p * BLK : (p + 1) * BLK, s * BLK : (s + 1) * BLK])
        rows.append(jnp.concatenate(parts, axis=1))
    return jnp.concatenate(rows, axis=0).astype(BF)


def enlarge(small, out_ref):
    rows = 4 * WB * 8
    up = jnp.where((iota((rows, 4 * WB), 0) >> 3) == iota((rows, 4 * WB), 1), 1.0, 0.0)
    out = jnp.where((iota((WB, DEPTH), 1) >> 3) == iota((WB, DEPTH), 0), 1.0, 0.0)
    tall = dot(up.astype(BF), small).astype(BF)
    wide = dot(tall, out.astype(BF))
    same = (iota((rows, DEPTH), 0) & 7) == (iota((rows, DEPTH), 1) & 7)
    out_ref[...] = jnp.where(same, wide, 0.0).astype(BF)


def own_ops_body(a_ref, wl_ref, wr_ref, b_ref, at_ref, kl_ref, kr_ref):
    for j in range(2):
        values = a_ref[j].astype(F32)
        for p in range(PHYS):
            b_ref[j, p] = spread(values[:, p * BLK : (p + 1) * BLK], p % 2)
        at_ref[j] = flipped(values[:, :128], 2)
    enlarge(wl_ref[...], kl_ref)
    enlarge(wr_ref[...], kr_ref)


def far_ops_body(a_ref, own_ref, b_ref, at_ref):
    for j in range(2):
        values = a_ref[j].astype(F32)
        for p in range(2):
            b_ref[j, p] = spread(values[:, p * BLK : (p + 1) * BLK], p)
        at_ref[j, :, :128] = own_ref[j]
        at_ref[j, :, 128:] = flipped(values, 2)


def raw_pair(ref, u, lt):
    lane = iota((BLK, 128), 1) < BLK
    if u == WB // 2:
        cols = slice(2 * u * BLK, WB * BLK)
        parts = [ref[2 * lt + i, :, cols].astype(F32) for i in range(2)]
        return jnp.concatenate(parts, axis=1), None
    low = ref[2 * lt, :, u * 128 : (u + 1) * 128].astype(F32)
    high = ref[2 * lt + 1, :, u * 128 : (u + 1) * 128].astype(F32)
    first = jnp.where(lane, low, pltpu.roll(high, BLK, 1))
    second = jnp.where(lane, pltpu.roll(low, BLK, 1), high)
    return first, second


def flat_pair(ref, u, lt):
    at = lt * HALF + 2 * u * 128
    first = ref[:, at : at + 128].astype(F32)
    if u == WB // 2:
        return first, None
    return first, ref[:, at + 128 : at + 256].astype(F32)


def flatten(env_ref, flat_ref):
    for lt in range(2):
        for u in range(9):
            at = lt * HALF + 2 * u * 128
            first, second = raw_pair(env_ref, u, lt)
            flat_ref[:, at : at + 128] = first.astype(BF)
            if second is not None:
                flat_ref[:, at + 128 : at + 256] = second.astype(BF)


def rows_of(flat_ref, e_ref):
    for lt in range(2):
        for w in range(WB):
            at = lt * HALF + w * 128
            e_ref[w * BLK : (w + 1) * BLK, lt * 128 : (lt + 1) * 128] = flat_ref[:, at : at + 128]


def woven(first, second):
    width = first.shape[-1]
    if second is None:
        second = jnp.zeros_like(first)
    parts = [first.reshape(GROUPS, 8, width), second.reshape(GROUPS, 8, width)]
    return jnp.concatenate(parts, axis=1).astype(BF)


def grouped(ref, m_ref):
    for lt in range(2):
        for u in range(9):
            both = woven(*flat_pair(ref, u, lt))
            m_ref[:, u * 16 : (u + 1) * 16, lt * 128 : (lt + 1) * 128] = both


def mixed(m_ref, k, count, h):
    low = dot(k, m_ref[2 * h]).reshape(count * WB, 8, 256)
    high = dot(k, m_ref[2 * h + 1]).reshape(count * WB, 8, 256)
    return jnp.concatenate([low, high], axis=1).astype(BF)


def left_states(e_ref, k_ref, k_at, b_ref, states, m_ref, y_ref, to):
    for p in range(states):
        inner = dot(e_ref[...], b_ref[p])
        for u in range(9):
            first = inner[2 * u * BLK : (2 * u + 1) * BLK]
            second = inner[(2 * u + 1) * BLK : (2 * u + 2) * BLK] if 2 * u + 1 < WB else None
            m_ref[p, :, u * 16 : (u + 1) * 16, :] = woven(first, second)
        k = k_ref[(k_at + p) * WB * 8 : (k_at + p + 1) * WB * 8]
        for h in range(4):
            out = mixed(m_ref.at[p], k, 1, h)
            rows = slice((to + p) * BLK + h * 16, (to + p) * BLK + (h + 1) * 16)
            for v in range(WB):
                for lt in range(2):
                    y_ref[rows, lt * HALF + v * 128 : lt * HALF + (v + 1) * 128] = out[
                        v, :, lt * 128 : (lt + 1) * 128
                    ]


def right_states(m_ref, k, b_ref, b_at, f_ref, y_ref, to):
    for h in range(4):
        f_ref[:, h * 16 : (h + 1) * 16, :] = mixed(m_ref, k, 2, h)
    for p in range(2):
        source = f_ref[p * WB : (p + 1) * WB].reshape(WB * BLK, 256)
        out = dot_t(source, b_ref[b_at + p]).astype(BF)
        rows = slice((to + p) * BLK, (to + p + 1) * BLK)
        for v in range(WB):
            for lt in range(2):
                y_ref[rows, lt * HALF + v * 128 : lt * HALF + (v + 1) * 128] = out[
                    v * BLK : (v + 1) * BLK, lt * 128 : (lt + 1) * 128
                ]


def closed(lhs_ref, own_ref, y_ref, out_ref):
    low = (iota((BLK, HALF), 1) & 127) < BLK
    for lt in range(2):
        cols = slice(lt * HALF, (lt + 1) * HALF)
        inner = jnp.concatenate([own_ref[:, cols], y_ref[:, cols]], axis=0)
        both = dot(lhs_ref[lt * 128 : (lt + 1) * 128, :], inner)
        out_ref[:, cols] = jnp.where(low, both[:BLK], both[BLK:]).astype(BF)


def left_half(flat_ref, k_ref, b_ref, y_ref, e_ref, m_ref):
    rows_of(flat_ref, e_ref)
    left_states(e_ref, k_ref, 0, b_ref, 2, m_ref, y_ref, 0)


def right_half(flat_ref, k_ref, b_ref, y_ref, m_ref, f_ref):
    grouped(flat_ref, m_ref)
    right_states(m_ref, k_ref[: 2 * WB * 8], b_ref, 0, f_ref, y_ref, 0)


def left_rest_raw(env_ref, k_ref, b_ref, own_ref, lhs_ref, out_ref, flat_ref, y_ref, e_ref, m_ref):
    flatten(env_ref, flat_ref)
    left_rest(flat_ref, k_ref, b_ref, own_ref, lhs_ref, out_ref, y_ref, e_ref, m_ref)


def left_rest(flat_ref, k_ref, b_ref, own_ref, lhs_ref, out_ref, y_ref, e_ref, m_ref):
    rows_of(flat_ref, e_ref)
    left_states(e_ref, k_ref, 2, b_ref, 2, m_ref, y_ref, 0)
    closed(lhs_ref, own_ref, y_ref, out_ref)


def right_rest_raw(env_ref, k_ref, b_ref, own_ref, lhs_ref, out_ref, flat_ref, y_ref, m_ref, f_ref):
    flatten(env_ref, flat_ref)
    right_rest(flat_ref, k_ref, b_ref, own_ref, lhs_ref, out_ref, y_ref, m_ref, f_ref)


def right_rest(flat_ref, k_ref, b_ref, own_ref, lhs_ref, out_ref, y_ref, m_ref, f_ref):
    grouped(flat_ref, m_ref)
    right_states(m_ref, k_ref[2 * WB * 8 :], b_ref, 2, f_ref, y_ref, 0)
    closed(lhs_ref, own_ref, y_ref, out_ref)


def prepare(left_hbm, right_hbm, a_ref, wl_ref, wr_ref, b_ref, at_ref, kl_ref, kr_ref, yl_ref, yr_ref, fl_ref, fr_ref, raw_ref, e_ref, m_ref, g_ref, f_ref, sems):
    copies = [
        pltpu.make_async_copy(source, raw_ref.at[i], sems.at[i])
        for i, source in enumerate((left_hbm, right_hbm))
    ]
    for copy in copies:
        copy.start()
    own_ops_body(a_ref, wl_ref, wr_ref, b_ref, at_ref, kl_ref, kr_ref)
    copies[0].wait()
    flatten(raw_ref.at[0], fl_ref)
    left_half(fl_ref, kl_ref, b_ref.at[0], yl_ref, e_ref, m_ref)
    copies[1].wait()
    flatten(raw_ref.at[1], fr_ref)
    right_half(fr_ref, kr_ref, b_ref.at[1], yr_ref, g_ref, f_ref)


LEFT_SCRATCH = [pltpu.VMEM((WB * BLK, 256), BF), pltpu.VMEM((2, GROUPS, DEPTH, 256), BF)]
RIGHT_SCRATCH = [pltpu.VMEM((GROUPS, DEPTH, 256), BF), pltpu.VMEM((2 * WB, BLK, 256), BF)]


def diagonal(ref, lt, g_ref):
    lane = (iota((BLK, HALF), 1) & 127) < BLK
    low = jnp.where(lane, 1.0, 0.0).astype(BF)
    high = jnp.where(lane, 0.0, 1.0).astype(BF)
    values = ref[:, lt * HALF : (lt + 1) * HALF]
    g_ref[:BLK, :] = values * low
    g_ref[BLK:, :] = values * high


def chosen(flag_ref, got_ref, edge_ref, g_ref):
    @pl.when(flag_ref[0] == 0)
    def _():
        for lt in range(2):
            diagonal(got_ref, lt, g_ref.at[lt])

    @pl.when(flag_ref[0] != 0)
    def _():
        for lt in range(2):
            diagonal(edge_ref, lt, g_ref.at[lt])


def squared(values):
    return jnp.sum((values * values).reshape(-1, 8, values.shape[1]), axis=0)


def first_body(flag_ref, got_ref, edge_ref, own_ref, far_ref, out_ref, sum_ref, g_ref):
    chosen(flag_ref, got_ref, edge_ref, g_ref)
    total = jnp.zeros((8, 256), F32)
    for lt in range(2):
        cols = slice(lt * HALF, (lt + 1) * HALF)
        inner = jnp.concatenate([own_ref[:, cols], far_ref[:, cols]], axis=0)
        out = dot_t(g_ref[lt], inner)
        out_ref[lt * 128 : (lt + 1) * 128, :] = out
        total = total + squared(out)
    sum_ref[...] = total[:, :128] + total[:, 128:]


def second_body(flag_ref, got_ref, edge_ref, y_ref, far_ref, sum_ref, own_ref, away_ref, sums_ref, g_ref):
    chosen(flag_ref, got_ref, edge_ref, g_ref)
    total = jnp.zeros((8, 128), F32)
    for lt in range(2):
        cols = slice(lt * HALF, (lt + 1) * HALF)
        inner = jnp.concatenate([y_ref[:, cols], far_ref[:, cols]], axis=0)
        out = dot_t(inner, g_ref[lt])
        own_ref[:, lt * 128 : (lt + 1) * 128] = out[:128]
        away_ref[:, lt * 128 : (lt + 1) * 128] = out[128:]
        total = total + squared(out)
    first = jnp.sum(sum_ref[...])
    sums_ref[...] = jnp.where(iota(sums_ref.shape, 1) < 4, first, jnp.sum(total))


def final_body(entries, first_ref, own_ref, away_ref, sums_ref, out_ref):
    total = jnp.sum(sums_ref[...], axis=0)
    scale = lax.rsqrt(total * (1.0 / entries) + 1e-06)
    for s in range(4):
        out_ref[0, s] = first_ref[s * BLK : (s + 1) * BLK, :] * scale[:1, :1]
        parts = []
        for p in range(PHYS):
            ref, at = (own_ref, p) if p < 2 else (away_ref, p - 2)
            t = target(s, p)
            parts.append(ref[at * BLK : (at + 1) * BLK, t * BLK : (t + 1) * BLK])
        out_ref[1, s] = jnp.concatenate(parts, axis=1) * scale[4:5, :1]


def passed_along(block, axis, distance):
    devices = lax.axis_size(axis)
    route = [(i, (i + distance) % devices) for i in range(devices)]
    return lax.ppermute(block, axis, route)


def shifted(value, axis, by):
    devices = lax.axis_size(axis)
    pairs = [(i, i + by) for i in range(devices) if 0 <= i + by < devices]
    return lax.ppermute(value, axis, pairs)


def local(mps, left_env, right_env, row_fill, col_fill, mpo_values, mpo_pattern):
    left_raw, right_raw = left_env[0], right_env[0]
    left_behind = passed_along(left_raw, "site", 1)
    right_ahead = passed_along(right_raw, "site", -1)
    weights = mpo_values * mpo_pattern.astype(BF)
    left_small = weights.transpose(2, 1, 0).reshape(PHYS * WB, WB)
    right_small = weights.transpose(2, 0, 1).reshape(PHYS * WB, WB)
    masked, high = call(
        keep_inside,
        [shape((2, 256, 256)), shape((2, 256, 128))],
        [
            pltpu.SMEM((2, 4), jnp.int32),
            pltpu.SMEM((2, 4, PHYS), jnp.int32),
            pltpu.VMEM((2, 4, BLK, 256), BF),
            pltpu.SemaphoreType.DMA((3,)),
        ],
        hbm=3,
        operands=(row_fill, col_fill, mps),
        mib=58,
    )
    high_behind = passed_along(high, "site", 1)
    rows = 4 * WB * 8
    part, flat = shape((128, FULL)), shape((BLK, FULL))
    blocks, turned_own, k_left, k_right, left_part, right_part, left_edge, right_edge = call(
        prepare,
        [
            shape((2, PHYS, 256, 256)),
            shape((2, 256, 128)),
            shape((rows, DEPTH)),
            shape((rows, DEPTH)),
            part,
            part,
            flat,
            flat,
        ],
        [
            pltpu.VMEM((2, 4, BLK, WB * BLK), BF),
            *LEFT_SCRATCH,
            *RIGHT_SCRATCH,
            pltpu.SemaphoreType.DMA((2,)),
        ],
        hbm=2,
        operands=(left_raw, right_raw, masked, left_small, right_small),
        mib=16,
    )
    whole = pltpu.VMEM((128, FULL), BF)
    kept = pltpu.VMEM((BLK, FULL), BF)
    far_blocks, turned = call(
        far_ops_body,
        [shape((2, 2, 256, 256)), shape((2, 256, 256))],
        operands=(high_behind, turned_own),
        after=(left_part, right_part, left_behind, right_ahead),
    )
    left_one = call(
        left_rest_raw,
        flat,
        [kept, whole, *LEFT_SCRATCH],
        operands=(left_behind, k_left, far_blocks[0], left_part, turned[0]),
        after=(right_part,),
    )
    left_one_behind = passed_along(left_one, "site", 1)
    right_one = call(
        right_rest_raw,
        flat,
        [kept, whole, *RIGHT_SCRATCH],
        operands=(right_ahead, k_right, blocks[1], right_part, masked[1]),
        after=(left_one,),
    )
    right_one_ahead = passed_along(right_one, "site", -1)
    left_part = call(
        left_half, part, LEFT_SCRATCH, operands=(left_one, k_left, blocks[1]), after=(right_one,)
    )
    right_part = call(right_half, part, RIGHT_SCRATCH, operands=(right_one, k_right, blocks[0]))
    left_out, left_far = call(
        left_rest,
        [flat, part],
        LEFT_SCRATCH,
        operands=(left_one_behind, k_left, far_blocks[1], left_part, turned[1]),
        after=(right_part,),
    )
    left_got = shifted(left_out, "sector", 1)
    right_out, right_far = call(
        right_rest,
        [flat, part],
        RIGHT_SCRATCH,
        operands=(right_one_ahead, k_right, blocks[0], right_part, masked[0]),
        after=(left_out,),
    )
    right_got = shifted(right_out, "sector", -1)
    position = lax.axis_index("sector")
    first_flag = (position == 0).astype(jnp.int32).reshape(1)
    last_flag = (position == lax.axis_size("sector") - 1).astype(jnp.int32).reshape(1)
    diag = pltpu.VMEM((2, 128, HALF), BF)
    first, first_sum = call(
        first_body,
        [shape((256, 256), F32), shape((8, 128), F32)],
        [diag],
        smem=1,
        operands=(first_flag, left_got, left_edge, right_part, right_far),
        after=(right_out,),
    )
    devices = lax.axis_size("site")
    own, away, sums = call(
        second_body,
        [shape((128, 256), F32), shape((128, 256), F32), shape((devices, 8, 128), F32)],
        [diag],
        smem=1,
        operands=(last_flag, right_got, right_edge, left_part, left_far, first_sum),
    )
    back = passed_along(away, "site", -1)
    gathered = lax.all_to_all(sums, "site", 0, 0, tiled=True)
    return call(
        functools.partial(final_body, 256 * 256 * devices),
        shape((2, 4, BLK, 256), F32),
        operands=(first, own, back, gathered),
    )


def solution(mesh):
    in_specs = (
        P("sector", "site", None, None),
        P("sector", "site", None, None),
        P("sector", "site", None, None),
        P("sector", "site"),
        P("sector", "site", None),
        P(),
        P(),
    )
    out_specs = P("sector", "site", None, None)
    return jax.shard_map(local, mesh=mesh, in_specs=in_specs, out_specs=out_specs, check_vma=False)
```

time: 75.2 us -> 69.7 us (0.927)
  starting transfers between devices: 21 us -> 16.7 us
  local copies, waits for them, and re-layouts: 7.3 us -> 4.69 us
  waiting for transfers between devices: 12.1 us -> 14.6 us
  Pallas kernels: 18.3 us -> 16.5 us
  blocking collectives: 15 us -> 16.6 us
  other arithmetic: 0.79 us -> 0.01 us
    ppermute x6, starting transfers between devices: 14 us -> 9.62 us  [passed_along(): return lax.ppermute(block, axis, route)]
    unnamed x26 -> x32, local copies, waits for them, and re-layouts: 6.91 us -> 4.3 us
    ppermute x2, waiting for transfers between devices: 8.04 us -> 10.1 us  [shifted(): return lax.ppermute(value, axis, pairs)]
    pallas_call x14 -> x12, Pallas kernels: 18.3 us -> 16.5 us  [call(): pl.pallas_call(ordered, out_shape=outs, in_specs=[pl.BlockSpec(memory_spa...]
    all_to_all x1, blocking collectives: 15 us -> 16.6 us  [local(): gathered = lax.all_to_all(sums, 'site', 0, 0, tiled=True)]
    transpose x1, other arithmetic: 0.79 us -> 0.01 us  [local(): right_small = weights.transpose(2, 0, 1).reshape(PHYS * WB, WB)]
  transfers between devices with their start and end apart: 8 -> 8, of which waited for: 3 -> 5; matrix products, arithmetic and copies ran while one was open for 2% -> 0% of each run, Pallas kernels for 22% -> 18%
where the time goes in v1:
time: 69.7 us; the launch traced here: 69.3 us
  starting transfers between devices  16.7 us (24%)
  blocking collectives  16.6 us (24%)
  Pallas kernels  16.5 us (24%)
  waiting for transfers between devices  14.6 us (21%)
  local copies, waits for them, and re-layouts  4.69 us (7%)
    all_to_all x1, blocking collectives, local(): gathered = lax.all_to_all(sums, 'site', 0, 0, tiled=True)  16.6 us
    pallas_call x12, Pallas kernels, call(): pl.pallas_call(ordered, out_shape=outs, in_specs=[pl.BlockSpec(memory_spa...  16.5 us
    ppermute x2, waiting for transfers between devices, shifted(): return lax.ppermute(value, axis, pairs)  10.1 us
    ppermute x6, starting transfers between devices, passed_along(): return lax.ppermute(block, axis, route)  9.62 us
    ppermute x2, starting transfers between devices, shifted(): return lax.ppermute(value, axis, pairs)  7.04 us
    ppermute x6, waiting for transfers between devices, passed_along(): return lax.ppermute(block, axis, route)  4.45 us
    unnamed x32, local copies, waits for them, and re-layouts  4.3 us
  transfers between devices with their start and end apart: 8, of which 5 were waited for; matrix products, arithmetic and copies ran while one was open for 0% of the time, Pallas kernels for 18%

profile of v1, /device:TPU:199, one launch (start us, length us, event | category | flops | bytes accessed | tf_op | source)
XLA Modules:
  0.0 69.3 jit_solution(11654237422275112846)
XLA Ops:
  0.0 1.9 %collective-permute-start = (bf16[4,64,1088]{2,1,0:T(8,128)(2,1)}, bf16[4,64,1088]{2,1,0:T(8,128)(2,1)S(1)}, u32[]{:S(2)}, u32[]{:S(2)}) collective-permute-start(bf16[4,64,1088]{2,1,0:T(8,128)(2,1)} %bitcast.26), channel_id=1, source_target_pairs={{0,32},{32,64},{64,96},{96,128},{128,160},{160,192},{192,224},{224... | collective-permute-start | bytes 1671176 | tf_op jit(solution)/shard_map/ppermute | solution.py:350
  1.9 0.0 copy-start.14
  1.9 0.0 copy-start.15
  1.9 0.0 copy-start.2
  1.9 0.0 copy-start.3
  1.9 0.0 collective-permute-start.2
  1.9 1.9 %shard_map.73 = (bf16[2,256,256]{2,1,0:T(8,128)(2,1)}, bf16[2,256,128]{2,1,0:T(8,128)(2,1)}) custom-call(s32[2,4]{1,0:T(2,128)} %refs_0_.1, s32[2,4,4]{2,1,0:T(4,128)} %refs_1_.1, bf16[2,4,64,256]{3,2,1,0:T(8,128)(2,1)} %refs_2_.1), custom_call_target="tpu_custom_call" | custom-call | flops 1320000000 | bytes 1 | tf_op jit(solution)/shard_map/pallas_call | solution.py:36
  3.8 1.6 %collective-permute-start.1 = (bf16[2,256,128]{2,1,0:T(8,128)(2,1)}, bf16[2,256,128]{2,1,0:T(8,128)(2,1)S(1)}, u32[]{:S(2)}, u32[]{:S(2)}) collective-permute-start(bf16[2,256,128]{2,1,0:T(8,128)(2,1)} %get-tuple-element.28), channel_id=1, source_target_pairs={{0,32},{32,64},{64,96},{96,128},{128,160},{160,192},{192,224},{224... | collective-permute-start | bytes 393224 | tf_op jit(solution)/shard_map/ppermute | solution.py:350
  5.4 0.0 copy-done.14
  5.4 0.0 copy-done.15
  5.5 0.1 reshape.18
  5.6 0.1 copy.11.refs_3_
  5.7 0.0 copy-done.2
  5.7 0.0 copy-done.3
  5.7 0.0 copy-start
  5.7 0.9 %copy-done = bf16[2,256,256]{2,1,0:T(8,128)(2,1)S(1)} copy-done((bf16[2,256,256]{2,1,0:T(8,128)(2,1)S(1)}, bf16[2,256,256]{2,1,0:T(8,128)(2,1)}, u32[]{:S(2)}) %copy-start) | copy-done | bytes 262168
  6.7 3.5 %shard_map.74 = (bf16[2,4,256,256]{3,2,1,0:T(8,128)(2,1)S(1)}, bf16[2,256,128]{2,1,0:T(8,128)(2,1)S(1)}, bf16[544,144]{1,0:T(8,128)(2,1)S(1)}, bf16[544,144]{1,0...) custom-call(bf16[4,64,1088]{2,1,0:T(8,128)(2,1)S(1)} %bitcast.27, ...), custom_call_target="tpu_custom_call" | custom-call | flops 1320000000 | bytes 1 | tf_op jit(solution)/shard_map/pallas_call | solution.py:36
  10.2 0.0 copy-start.6
  10.2 0.0 copy-start.12
  10.2 0.1 slice_bitcast_fusion
  10.3 0.1 collective-permute-done.1.refs_0_
  10.4 0.0 collective-permute-done.refs_4_.refs_0_
  10.4 1.3 %collective-permute-done.2.refs_5_.refs_0_ = bf16[4,64,1088]{2,1,0:T(8,128)(2,1)S(1)} collective-permute-done((bf16[4,64,1088]{2,1,0:T(8,128)(2,1)}, bf16[4,64,1088]{2,1,0:T(8,128)(2,1)S(1)}, u32[]{:S(2)}, u32[]{:S(2)}) %collective-permute-start.2) | collective-permute-done | bytes 557088 | tf_op jit(solution)/shard_map/ppermute | solution.py:350
  11.7 0.4 shard_map.75
  12.1 0.0 copy-done.6
  12.1 0.0 copy-done.12
  12.2 0.0 copy-start.1
  12.2 1.8 %shard_map.76.refs_5_.refs_0_ = bf16[64,4352]{1,0:T(8,128)(2,1)S(1)} custom-call(bf16[4,64,1088]{2,1,0:T(8,128)(2,1)S(1)} %collective-permute-done.refs_4_.refs_0_, bf16[544,144]{1,0:T(8,128)(2,1)S(1)} %get-tuple-element.27.refs_1_, bf16[2,256,256]{2,1,0:T(8,128)(2,1)S(1)} %get-tuple-element.50.refs_2_, ...), custom_call_target="tpu_custom_call" | custom-call | flops 1320000000 | bytes 1 | tf_op jit(solution)/shard_map/pallas_call | solution.py:36
  13.9 1.1 %collective-permute-start.3 = (bf16[64,4352]{1,0:T(8,128)(2,1)S(1)}, bf16[64,4352]{1,0:T(8,128)(2,1)S(1)}, u32[]{:S(2)}, u32[]{:S(2)}) collective-permute-start(bf16[64,4352]{1,0:T(8,128)(2,1)S(1)} %shard_map.76.refs_5_.refs_0_), channel_id=1, source_target_pairs={{0,32},{32,64},{64,96},{96,128},{128,160},{160,192},{192,224},{224... | collective-permute-start | bytes 1671176 | tf_op jit(solution)/shard_map/ppermute | solution.py:350
  15.0 0.0 copy-done.1
  15.1 1.4 %shard_map.77.refs_3_.refs_0_ = bf16[64,4352]{1,0:T(8,128)(2,1)S(1)} custom-call(bf16[4,64,1088]{2,1,0:T(8,128)(2,1)S(1)} %collective-permute-done.2.refs_5_.refs_0_, bf16[544,144]{1,0:T(8,128)(2,1)S(1)} %get-tuple-element.35.refs_1_, bf16[4,256,256]{2,1,0:T(8,128)(2,1)S(1)} %get-tuple-element.48.refs_2_, ...), custom_call_target="tpu_custom_call" | custom-call | flops 1320000000 | bytes 1 | tf_op jit(solution)/shard_map/pallas_call | solution.py:36
  16.4 0.1 collective-permute-start.5
  16.5 1.1 %shard_map.78.refs_3_ = bf16[128,4352]{1,0:T(8,128)(2,1)S(1)} custom-call(bf16[64,4352]{1,0:T(8,128)(2,1)S(1)} %shard_map.76.refs_5_.refs_0_, bf16[544,144]{1,0:T(8,128)(2,1)S(1)} %get-tuple-element.27.refs_1_, bf16[4,256,256]{2,1,0:T(8,128)(2,1)S(1)} %get-tuple-element.48.refs_2_, bf16[64,4352]{1,0:T(8,128)(2,1)S(1)} %shard_map.77.refs_3_.refs_0_), custom_call_target="tpu_custom_call" | custom-call | flops 1320000000 | bytes 1 | tf_op jit(solution)/shard_map/pallas_call | solution.py:36
  17.6 0.0 copy-start.8
  17.6 0.9 %shard_map.79.refs_5_.refs_3_ = bf16[128,4352]{1,0:T(8,128)(2,1)S(1)} custom-call(bf16[64,4352]{1,0:T(8,128)(2,1)S(1)} %shard_map.77.refs_3_.refs_0_, bf16[544,144]{1,0:T(8,128)(2,1)S(1)} %get-tuple-element.35.refs_1_, bf16[4,256,256]{2,1,0:T(8,128)(2,1)S(1)} %get-tuple-element.47.refs_2_), custom_call_target="tpu_custom_call" | custom-call | flops 1320000000 | bytes 1 | tf_op jit(solution)/shard_map/pallas_call | solution.py:36
  18.5 3.0 %collective-permute-done.3.refs_0_ = bf16[64,4352]{1,0:T(8,128)(2,1)S(1)} collective-permute-done((bf16[64,4352]{1,0:T(8,128)(2,1)S(1)}, bf16[64,4352]{1,0:T(8,128)(2,1)S(1)}, u32[]{:S(2)}, u32[]{:S(2)}) %collective-permute-start.3) | collective-permute-done | bytes 557088 | tf_op jit(solution)/shard_map/ppermute | solution.py:350
  21.5 0.0 copy-done.8
  21.5 1.6 %shard_map.80 = (bf16[64,4352]{1,0:T(8,128)(2,1)S(1)}, bf16[128,4352]{1,0:T(8,128)(2,1)S(1)}) custom-call(bf16[64,4352]{1,0:T(8,128)(2,1)S(1)} %collective-permute-done.3.refs_0_, bf16[544,144]{1,0:T(8,128)(2,1)S(1)} %get-tuple-element.27.refs_1_, bf16[2,256,256]{2,1,0:T(8,128)(2,1)S(1)} %get-tuple-element.49.refs_2_, ...), custom_call_target="tpu_custom_call" | custom-call | flops 1320000000 | bytes 1 | tf_op jit(solution)/shard_map/pallas_call | solution.py:36
  23.1 0.0 copy-start.10
  23.1 5.1 %collective-permute-start.4 = (bf16[64,4352]{1,0:T(8,128)(2,1)S(1)}, bf16[64,4352]{1,0:T(8,128)(2,1)S(1)}, u32[]{:S(2)}, u32[]{:S(2)}) collective-permute-start(bf16[64,4352]{1,0:T(8,128)(2,1)S(1)} %get-tuple-element.36.refs_5_), channel_id=1, source_target_pairs={{0,1},{1,2},{2,3},{3,4},{4,5},{5,6},{6,7},{7,8},{8,9},{9,10},{10,1... | collective-permute-start | bytes 1671176 | tf_op jit(solution)/shard_map/ppermute | solution.py:356
  28.3 0.0 collective-permute-done.5.refs_0_
  28.3 1.2 %shard_map.81 = (bf16[64,4352]{1,0:T(8,128)(2,1)S(1)}, bf16[128,4352]{1,0:T(8,128)(2,1)S(1)}) custom-call(bf16[64,4352]{1,0:T(8,128)(2,1)S(1)} %collective-permute-done.5.refs_0_, bf16[544,144]{1,0:T(8,128)(2,1)S(1)} %get-tuple-element.35.refs_1_, bf16[4,256,256]{2,1,0:T(8,128)(2,1)S(1)} %get-tuple-element.47.refs_2_, ...), custom_call_target="tpu_custom_call" | custom-call | flops 1320000000 | bytes 1 | tf_op jit(solution)/shard_map/pallas_call | solution.py:36
  29.5 0.0 copy-done.10
  29.5 0.0 copy-start.4
  29.5 1.0 %copy-done.4 = bf16[128,4352]{1,0:T(8,128)(2,1)} copy-done((bf16[128,4352]{1,0:T(8,128)(2,1)}, bf16[128,4352]{1,0:T(8,128)(2,1)S(1)}, u32[]{:S(2)}) %copy-start.4) | copy-done | bytes 1114136
  30.5 1.9 %collective-permute-start.6 = (bf16[64,4352]{1,0:T(8,128)(2,1)S(1)}, bf16[64,4352]{1,0:T(8,128)(2,1)S(1)}, u32[]{:S(2)}, u32[]{:S(2)}) collective-permute-start(bf16[64,4352]{1,0:T(8,128)(2,1)S(1)} %get-tuple-element.39.refs_5_), channel_id=1, source_target_pairs={{1,0},{2,1},{3,2},{4,3},{5,4},{6,5},{7,6},{8,7},{9,8},{10,9},{11,1... | collective-permute-start | bytes 1671176 | tf_op jit(solution)/shard_map/ppermute | solution.py:356
  32.4 4.0 %collective-permute-done.4.refs_1_ = bf16[64,4352]{1,0:T(8,128)(2,1)S(1)} collective-permute-done((bf16[64,4352]{1,0:T(8,128)(2,1)S(1)}, bf16[64,4352]{1,0:T(8,128)(2,1)S(1)}, u32[]{:S(2)}, u32[]{:S(2)}) %collective-permute-start.4) | collective-permute-done | bytes 557088 | tf_op jit(solution)/shard_map/ppermute | solution.py:356
  36.4 0.0 copy-start.5
  36.4 1.2 %copy-done.5 = bf16[128,4352]{1,0:T(8,128)(2,1)S(1)} copy-done((bf16[128,4352]{1,0:T(8,128)(2,1)S(1)}, bf16[128,4352]{1,0:T(8,128)(2,1)}, u32[]{:S(2)}) %copy-start.5) | copy-done | bytes 1114136
  37.7 0.0 copy-start.7
  37.7 1.1 %copy-done.7 = bf16[64,4352]{1,0:T(8,128)(2,1)S(1)} copy-done((bf16[64,4352]{1,0:T(8,128)(2,1)S(1)}, bf16[64,4352]{1,0:T(8,128)(2,1)}, u32[]{:S(2)}) %copy-start.7) | copy-done | bytes 557080
  38.7 0.0 copy-start.9
  38.7 0.0 copy-start.11
  38.7 0.0 copy-start.13
  38.7 0.9 %shard_map.82 = (f32[256,256]{1,0:T(8,128)S(1)}, f32[8,128]{1,0:T(8,128)S(1)}) custom-call(s32[1]{0:T(128)} %bitcast.refs_0_, bf16[64,4352]{1,0:T(8,128)(2,1)S(1)} %collective-permute-done.4.refs_1_, bf16[64,4352]{1,0:T(8,128)(2,1)S(1)} %copy-done.7, bf16[128,4352]{1,0:T(8,128)(2,1)S(1)} %shard_map.79.refs_5_.refs_3_, bf16[128,4352]{1,0:T(8,128)(2,1)S(1)} %copy-done.5, ...), custom_call_target="tpu_custom_call" | custom-call | flops 1320000000 | bytes 1 | tf_op jit(solution)/shard_map/pallas_call | solution.py:36
  39.7 6.1 %collective-permute-done.6.refs_1_ = bf16[64,4352]{1,0:T(8,128)(2,1)S(1)} collective-permute-done((bf16[64,4352]{1,0:T(8,128)(2,1)S(1)}, bf16[64,4352]{1,0:T(8,128)(2,1)S(1)}, u32[]{:S(2)}, u32[]{:S(2)}) %collective-permute-start.6) | collective-permute-done | bytes 557088 | tf_op jit(solution)/shard_map/ppermute | solution.py:356
  45.8 0.0 copy-done.9
  45.8 0.0 copy-done.11
  45.8 0.0 copy-done.13
  45.8 1.0 %shard_map.83 = (f32[128,256]{1,0:T(8,128)S(1)}, f32[128,256]{1,0:T(8,128)S(1)}, f32[16,8,128]{2,1,0:T(8,128)S(1)}) custom-call(s32[1]{0:T(128)} %bitcast.13.refs_0_, bf16[64,4352]{1,0:T(8,128)(2,1)S(1)} %collective-permute-done.6.refs_1_, bf16[64,4352]{1,0:T(8,128)(2,1)S(1)} %copy-done.13, bf16[128,4352]{1,0:T(8,128)(2,1)S(1)} %copy-done.9, ...), custom_call_target="tpu_custom_call" | custom-call | flops 1320000000 | bytes 1 | tf_op jit(solution)/shard_map/pallas_call | solution.py:36
  46.8 4.9 %collective-permute-start.7 = (f32[128,256]{1,0:T(8,128)S(1)}, f32[128,256]{1,0:T(8,128)S(1)}, u32[]{:S(2)}, u32[]{:S(2)}) collective-permute-start(f32[128,256]{1,0:T(8,128)S(1)} %get-tuple-element.45), channel_id=1, source_target_pairs={{0,480},{32,0},{64,32},{96,64},{128,96},{160,128},{192,160},{224,1... | collective-permute-start | bytes 393224 | tf_op jit(solution)/shard_map/ppermute | solution.py:350
  51.8 16.6 %all_to_all.5.refs_3_ = f32[16,8,128]{2,1,0:T(8,128)S(1)} all-to-all(f32[16,8,128]{2,1,0:T(8,128)S(1)} %get-tuple-element.46), channel_id=1, replica_groups=mesh['site'=16,'sector'=32] {'site'}, dimensions={0} | all-to-all | bytes 131072 | tf_op jit(solution)/shard_map/all_to_all | solution.py:469
  68.4 0.0 collective-permute-done.7.refs_2_
  68.4 0.9 %shard_map.84 = f32[2,4,64,256]{3,2,1,0:T(8,128)} custom-call(f32[256,256]{1,0:T(8,128)S(1)} %get-tuple-element.40.refs_0_, f32[128,256]{1,0:T(8,128)S(1)} %get-tuple-element.44.refs_1_, f32[128,256]{1,0:T(8,128)S(1)} %collective-permute-done.7.refs_2_, f32[16,8,128]{2,1,0:T(8,128)S(1)} %all_to_all.5.refs_3_), custom_call_target="tpu_custom_call" | custom-call | flops 1320000000 | bytes 1 | tf_op jit(solution)/shard_map/pallas_call | solution.py:36
  (6 shorter events, 0.1 us)
Async XLA Ops:
  0.0 10.4 %collective-permute-start = (bf16[4,64,1088]{2,1,0:T(8,128)(2,1)}, bf16[4,64,1088]{2,1,0:T(8,128)(2,1)S(1)}, u32[]{:S(2)}, u32[]{:S(2)}) collective-permute-start(bf16[4,64,1088]{2,1,0:T(8,128)(2,1)} %bitcast.26), channel_id=1, source_target_pairs={{0,32},{32,64},{64,96},{96,128},{128,160},{160,192},{192,224},{224... | collective-permute-start | bytes 1671176 | tf_op jit(solution)/shard_map/ppermute | solution.py:350
  1.9 3.6 %copy-start.14 = (s32[17,17,4]{1,2,0:T(4,128)S(1)}, s32[17,17,4]{1,2,0:T(4,128)}, u32[]{:S(2)}) copy-start(s32[17,17,4]{1,2,0:T(4,128)} %param.13) | copy-start | bytes 13876
  1.9 3.6 %copy-start.15 = (bf16[17,17,4]{1,2,0:T(4,128)(2,1)S(1)}, bf16[17,17,4]{1,2,0:T(4,128)(2,1)}, u32[]{:S(2)}) copy-start(bf16[17,17,4]{1,2,0:T(4,128)(2,1)} %param.12) | copy-start | bytes 6940
  1.9 3.9 %copy-start.2 = (bf16[1,4,64,1088]{3,2,1,0:T(8,128)(2,1)S(1)}, bf16[1,4,64,1088]{3,2,1,0:T(8,128)(2,1)}, u32[]{:S(2)}) copy-start(bf16[1,4,64,1088]{3,2,1,0:T(8,128)(2,1)} %param.8) | copy-start | bytes 1671172
  1.9 3.9 %copy-start.3 = (bf16[1,4,64,1088]{3,2,1,0:T(8,128)(2,1)S(1)}, bf16[1,4,64,1088]{3,2,1,0:T(8,128)(2,1)}, u32[]{:S(2)}) copy-start(bf16[1,4,64,1088]{3,2,1,0:T(8,128)(2,1)} %param.9) | copy-start | bytes 1671172
  1.9 9.8 %collective-permute-start.2 = (bf16[4,64,1088]{2,1,0:T(8,128)(2,1)}, bf16[4,64,1088]{2,1,0:T(8,128)(2,1)S(1)}, u32[]{:S(2)}, u32[]{:S(2)}) collective-permute-start(bf16[4,64,1088]{2,1,0:T(8,128)(2,1)} %bitcast.28), channel_id=1, source_target_pairs={{0,480},{32,0},{64,32},{96,64},{128,96},{160,128},{192,160},{224,1... | collective-permute-start | bytes 1671176 | tf_op jit(solution)/shard_map/ppermute | solution.py:350
  3.8 6.6 %collective-permute-start.1 = (bf16[2,256,128]{2,1,0:T(8,128)(2,1)}, bf16[2,256,128]{2,1,0:T(8,128)(2,1)S(1)}, u32[]{:S(2)}, u32[]{:S(2)}) collective-permute-start(bf16[2,256,128]{2,1,0:T(8,128)(2,1)} %get-tuple-element.28), channel_id=1, source_target_pairs={{0,32},{32,64},{64,96},{96,128},{128,160},{160,192},{192,224},{224... | collective-permute-start | bytes 393224 | tf_op jit(solution)/shard_map/ppermute | solution.py:350
  5.7 1.0 %copy-start = (bf16[2,256,256]{2,1,0:T(8,128)(2,1)S(1)}, bf16[2,256,256]{2,1,0:T(8,128)(2,1)}, u32[]{:S(2)}) copy-start(bf16[2,256,256]{2,1,0:T(8,128)(2,1)} %get-tuple-element.26.refs_2_) | copy-start | bytes 786436
  10.2 1.9 %copy-start.6 = (bf16[64,4352]{1,0:T(8,128)(2,1)}, bf16[64,4352]{1,0:T(8,128)(2,1)S(1)}, u32[]{:S(2)}) copy-start(bf16[64,4352]{1,0:T(8,128)(2,1)S(1)} %get-tuple-element.37.refs_2_) | copy-start | bytes 1671172
  10.2 1.9 %copy-start.12 = (bf16[64,4352]{1,0:T(8,128)(2,1)}, bf16[64,4352]{1,0:T(8,128)(2,1)S(1)}, u32[]{:S(2)}) copy-start(bf16[64,4352]{1,0:T(8,128)(2,1)S(1)} %get-tuple-element.41.refs_2_) | copy-start | bytes 1671172
  12.2 2.9 %copy-start.1 = (bf16[2,256,256]{2,1,0:T(8,128)(2,1)S(1)}, bf16[2,256,256]{2,1,0:T(8,128)(2,1)}, u32[]{:S(2)}) copy-start(bf16[2,256,256]{2,1,0:T(8,128)(2,1)} %get-tuple-element.26.refs_2_) | copy-start | bytes 786436
  13.9 7.6 %collective-permute-start.3 = (bf16[64,4352]{1,0:T(8,128)(2,1)S(1)}, bf16[64,4352]{1,0:T(8,128)(2,1)S(1)}, u32[]{:S(2)}, u32[]{:S(2)}) collective-permute-start(bf16[64,4352]{1,0:T(8,128)(2,1)S(1)} %shard_map.76.refs_5_.refs_0_), channel_id=1, source_target_pairs={{0,32},{32,64},{64,96},{96,128},{128,160},{160,192},{192,224},{224... | collective-permute-start | bytes 1671176 | tf_op jit(solution)/shard_map/ppermute | solution.py:350
  16.4 11.8 %collective-permute-start.5 = (bf16[64,4352]{1,0:T(8,128)(2,1)S(1)}, bf16[64,4352]{1,0:T(8,128)(2,1)S(1)}, u32[]{:S(2)}, u32[]{:S(2)}) collective-permute-start(bf16[64,4352]{1,0:T(8,128)(2,1)S(1)} %shard_map.77.refs_3_.refs_0_), channel_id=1, source_target_pairs={{0,480},{32,0},{64,32},{96,64},{128,96},{160,128},{192,160},{224,1... | collective-permute-start | bytes 1671176 | tf_op jit(solution)/shard_map/ppermute | solution.py:350
  17.6 3.9 %copy-start.8 = (bf16[128,4352]{1,0:T(8,128)(2,1)}, bf16[128,4352]{1,0:T(8,128)(2,1)S(1)}, u32[]{:S(2)}) copy-start(bf16[128,4352]{1,0:T(8,128)(2,1)S(1)} %shard_map.78.refs_3_) | copy-start | bytes 3342340
  23.1 6.4 %copy-start.10 = (bf16[128,4352]{1,0:T(8,128)(2,1)}, bf16[128,4352]{1,0:T(8,128)(2,1)S(1)}, u32[]{:S(2)}) copy-start(bf16[128,4352]{1,0:T(8,128)(2,1)S(1)} %get-tuple-element.42.refs_4_) | copy-start | bytes 3342340
  23.1 13.3 %collective-permute-start.4 = (bf16[64,4352]{1,0:T(8,128)(2,1)S(1)}, bf16[64,4352]{1,0:T(8,128)(2,1)S(1)}, u32[]{:S(2)}, u32[]{:S(2)}) collective-permute-start(bf16[64,4352]{1,0:T(8,128)(2,1)S(1)} %get-tuple-element.36.refs_5_), channel_id=1, source_target_pairs={{0,1},{1,2},{2,3},{3,4},{4,5},{5,6},{6,7},{7,8},{8,9},{9,10},{10,1... | collective-permute-start | bytes 1671176 | tf_op jit(solution)/shard_map/ppermute | solution.py:356
  29.5 1.0 %copy-start.4 = (bf16[128,4352]{1,0:T(8,128)(2,1)}, bf16[128,4352]{1,0:T(8,128)(2,1)S(1)}, u32[]{:S(2)}) copy-start(bf16[128,4352]{1,0:T(8,128)(2,1)S(1)} %get-tuple-element.38.refs_4_) | copy-start | bytes 3342340
  30.5 15.3 %collective-permute-start.6 = (bf16[64,4352]{1,0:T(8,128)(2,1)S(1)}, bf16[64,4352]{1,0:T(8,128)(2,1)S(1)}, u32[]{:S(2)}, u32[]{:S(2)}) collective-permute-start(bf16[64,4352]{1,0:T(8,128)(2,1)S(1)} %get-tuple-element.39.refs_5_), channel_id=1, source_target_pairs={{1,0},{2,1},{3,2},{4,3},{5,4},{6,5},{7,6},{8,7},{9,8},{10,9},{11,1... | collective-permute-start | bytes 1671176 | tf_op jit(solution)/shard_map/ppermute | solution.py:356
  36.4 1.2 %copy-start.5 = (bf16[128,4352]{1,0:T(8,128)(2,1)S(1)}, bf16[128,4352]{1,0:T(8,128)(2,1)}, u32[]{:S(2)}) copy-start(bf16[128,4352]{1,0:T(8,128)(2,1)} %copy-done.4) | copy-start | bytes 3342340
  37.7 1.1 %copy-start.7 = (bf16[64,4352]{1,0:T(8,128)(2,1)S(1)}, bf16[64,4352]{1,0:T(8,128)(2,1)}, u32[]{:S(2)}) copy-start(bf16[64,4352]{1,0:T(8,128)(2,1)} %copy-done.6) | copy-start | bytes 1671172
  38.7 7.1 %copy-start.9 = (bf16[128,4352]{1,0:T(8,128)(2,1)S(1)}, bf16[128,4352]{1,0:T(8,128)(2,1)}, u32[]{:S(2)}) copy-start(bf16[128,4352]{1,0:T(8,128)(2,1)} %copy-done.8) | copy-start | bytes 3342340
  38.7 7.1 %copy-start.11 = (bf16[128,4352]{1,0:T(8,128)(2,1)S(1)}, bf16[128,4352]{1,0:T(8,128)(2,1)}, u32[]{:S(2)}) copy-start(bf16[128,4352]{1,0:T(8,128)(2,1)} %copy-done.10) | copy-start | bytes 3342340
  38.7 7.1 %copy-start.13 = (bf16[64,4352]{1,0:T(8,128)(2,1)S(1)}, bf16[64,4352]{1,0:T(8,128)(2,1)}, u32[]{:S(2)}) copy-start(bf16[64,4352]{1,0:T(8,128)(2,1)} %copy-done.12) | copy-start | bytes 1671172
  46.8 21.5 %collective-permute-start.7 = (f32[128,256]{1,0:T(8,128)S(1)}, f32[128,256]{1,0:T(8,128)S(1)}, u32[]{:S(2)}, u32[]{:S(2)}) collective-permute-start(f32[128,256]{1,0:T(8,128)S(1)} %get-tuple-element.45), channel_id=1, source_target_pairs={{0,480},{32,0},{64,32},{96,64},{128,96},{160,128},{192,160},{224,1... | collective-permute-start | bytes 393224 | tf_op jit(solution)/shard_map/ppermute | solution.py:350

commit v2 on v1

--- a/solution.py
+++ b/solution.py
@@ -19,7 +19,7 @@
 
 
 def shape(dims, dtype=BF):
-    return jax.ShapeDtypeStruct(dims, dtype)
+    return pltpu.VMEM(dims, dtype)
 
 
 def call(body, outs, scratch=(), smem=0, hbm=0, operands=(), after=(), mib=16, us=1.20):
@@ -27,8 +27,15 @@
     spaces += [pltpu.VMEM] * (len(operands) - len(spaces))
     spaces += [pl.ANY] * len(after)
     single = not isinstance(outs, (list, tuple))
-    out_spec = pl.BlockSpec(memory_space=pltpu.VMEM)
+    out_specs = [
+        pl.BlockSpec(memory_space=pltpu.HBM if getattr(out, "memory_space", None) == pltpu.HBM else pltpu.VMEM)
+        for out in ([outs] if single else outs)
+    ]
     count = len(operands)
+    placed = [
+        pltpu.with_memory_space_constraint(value, space) if space == pltpu.HBM else value
+        for value, space in zip(operands, spaces)
+    ]
 
     def ordered(*refs):
         body(*refs[:count], *refs[count + len(after) :])
@@ -37,11 +44,11 @@
         ordered,
         out_shape=outs,
         in_specs=[pl.BlockSpec(memory_space=space) for space in spaces],
-        out_specs=out_spec if single else [out_spec] * len(outs),
+        out_specs=out_specs[0] if single else out_specs,
         scratch_shapes=list(scratch),
         compiler_params=pltpu.CompilerParams(vmem_limit_bytes=mib * 1024 * 1024),
         cost_estimate=pl.CostEstimate(flops=int(us * 1.1e9), bytes_accessed=1, transcendentals=0),
-    )(*operands, *after)
+    )(*placed, *after)
 
 
 def iota(dims, axis):
@@ -260,7 +267,7 @@
     closed(lhs_ref, own_ref, y_ref, out_ref)
 
 
-def prepare(left_hbm, right_hbm, a_ref, wl_ref, wr_ref, b_ref, at_ref, kl_ref, kr_ref, yl_ref, yr_ref, fl_ref, fr_ref, raw_ref, e_ref, m_ref, g_ref, f_ref, sems):
+def prepare(left_hbm, right_hbm, a_ref, wl_ref, wr_ref, b_ref, at_ref, kl_ref, kr_ref, yl_ref, yr_ref, raw_ref, flat_ref, e_ref, m_ref, g_ref, f_ref, sems):
     copies = [
         pltpu.make_async_copy(source, raw_ref.at[i], sems.at[i])
         for i, source in enumerate((left_hbm, right_hbm))
@@ -269,11 +276,11 @@
         copy.start()
     own_ops_body(a_ref, wl_ref, wr_ref, b_ref, at_ref, kl_ref, kr_ref)
     copies[0].wait()
-    flatten(raw_ref.at[0], fl_ref)
-    left_half(fl_ref, kl_ref, b_ref.at[0], yl_ref, e_ref, m_ref)
+    flatten(raw_ref.at[0], flat_ref.at[0])
+    left_half(flat_ref.at[0], kl_ref, b_ref.at[0], yl_ref, e_ref, m_ref)
     copies[1].wait()
-    flatten(raw_ref.at[1], fr_ref)
-    right_half(fr_ref, kr_ref, b_ref.at[1], yr_ref, g_ref, f_ref)
+    flatten(raw_ref.at[1], flat_ref.at[1])
+    right_half(flat_ref.at[1], kr_ref, b_ref.at[1], yr_ref, g_ref, f_ref)
 
 
 LEFT_SCRATCH = [pltpu.VMEM((WB * BLK, 256), BF), pltpu.VMEM((2, GROUPS, DEPTH, 256), BF)]
@@ -289,7 +296,7 @@
     g_ref[BLK:, :] = values * high
 
 
-def chosen(flag_ref, got_ref, edge_ref, g_ref):
+def chosen(flag_ref, edge_hbm, got_ref, raw_ref, flat_ref, g_ref, sem):
     @pl.when(flag_ref[0] == 0)
     def _():
         for lt in range(2):
@@ -297,16 +304,20 @@
 
     @pl.when(flag_ref[0] != 0)
     def _():
+        fetched = pltpu.make_async_copy(edge_hbm, raw_ref, sem)
+        fetched.start()
+        fetched.wait()
+        flatten(raw_ref, flat_ref)
         for lt in range(2):
-            diagonal(edge_ref, lt, g_ref.at[lt])
+            diagonal(flat_ref, lt, g_ref.at[lt])
 
 
 def squared(values):
     return jnp.sum((values * values).reshape(-1, 8, values.shape[1]), axis=0)
 
 
-def first_body(flag_ref, got_ref, edge_ref, own_ref, far_ref, out_ref, sum_ref, g_ref):
-    chosen(flag_ref, got_ref, edge_ref, g_ref)
+def first_body(flag_ref, edge_hbm, got_ref, own_ref, far_ref, sum_ref, out_ref, sums_ref, raw_ref, flat_ref, g_ref, sem):
+    chosen(flag_ref, edge_hbm, got_ref, raw_ref, flat_ref, g_ref, sem)
     total = jnp.zeros((8, 256), F32)
     for lt in range(2):
         cols = slice(lt * HALF, (lt + 1) * HALF)
@@ -314,11 +325,12 @@
         out = dot_t(g_ref[lt], inner)
         out_ref[lt * 128 : (lt + 1) * 128, :] = out
         total = total + squared(out)
-    sum_ref[...] = total[:, :128] + total[:, 128:]
-
-
-def second_body(flag_ref, got_ref, edge_ref, y_ref, far_ref, sum_ref, own_ref, away_ref, sums_ref, g_ref):
-    chosen(flag_ref, got_ref, edge_ref, g_ref)
+    second = jnp.sum(sum_ref[...])
+    sums_ref[...] = jnp.where(iota(sums_ref.shape, 1) < 4, jnp.sum(total), second)
+
+
+def second_body(flag_ref, edge_hbm, got_ref, y_ref, far_ref, own_ref, away_ref, sum_ref, raw_ref, flat_ref, g_ref, sem):
+    chosen(flag_ref, edge_hbm, got_ref, raw_ref, flat_ref, g_ref, sem)
     total = jnp.zeros((8, 128), F32)
     for lt in range(2):
         cols = slice(lt * HALF, (lt + 1) * HALF)
@@ -327,8 +339,7 @@
         own_ref[:, lt * 128 : (lt + 1) * 128] = out[:128]
         away_ref[:, lt * 128 : (lt + 1) * 128] = out[128:]
         total = total + squared(out)
-    first = jnp.sum(sum_ref[...])
-    sums_ref[...] = jnp.where(iota(sums_ref.shape, 1) < 4, first, jnp.sum(total))
+    sum_ref[...] = total
 
 
 def final_body(entries, first_ref, own_ref, away_ref, sums_ref, out_ref):
@@ -374,12 +385,11 @@
         ],
         hbm=3,
         operands=(row_fill, col_fill, mps),
-        mib=58,
     )
     high_behind = passed_along(high, "site", 1)
     rows = 4 * WB * 8
     part, flat = shape((128, FULL)), shape((BLK, FULL))
-    blocks, turned_own, k_left, k_right, left_part, right_part, left_edge, right_edge = call(
+    blocks, turned_own, k_left, k_right, left_part, right_part = call(
         prepare,
         [
             shape((2, PHYS, 256, 256)),
@@ -388,11 +398,10 @@
             shape((rows, DEPTH)),
             part,
             part,
-            flat,
-            flat,
         ],
         [
             pltpu.VMEM((2, 4, BLK, WB * BLK), BF),
+            pltpu.VMEM((2, BLK, FULL), BF),
             *LEFT_SCRATCH,
             *RIGHT_SCRATCH,
             pltpu.SemaphoreType.DMA((2,)),
@@ -403,73 +412,77 @@
     )
     whole = pltpu.VMEM((128, FULL), BF)
     kept = pltpu.VMEM((BLK, FULL), BF)
+    right_one = call(
+        right_rest_raw,
+        flat,
+        [kept, whole, *RIGHT_SCRATCH],
+        operands=(right_ahead, k_right, blocks[1], right_part, masked[1]),
+        after=(left_part,),
+    )
+    right_one_ahead = passed_along(right_one, "site", -1)
     far_blocks, turned = call(
         far_ops_body,
         [shape((2, 2, 256, 256)), shape((2, 256, 256))],
         operands=(high_behind, turned_own),
-        after=(left_part, right_part, left_behind, right_ahead),
+        after=(right_one, left_behind),
+        us=0.4,
     )
     left_one = call(
         left_rest_raw,
         flat,
         [kept, whole, *LEFT_SCRATCH],
         operands=(left_behind, k_left, far_blocks[0], left_part, turned[0]),
-        after=(right_part,),
+        after=(right_one,),
     )
     left_one_behind = passed_along(left_one, "site", 1)
-    right_one = call(
-        right_rest_raw,
-        flat,
-        [kept, whole, *RIGHT_SCRATCH],
-        operands=(right_ahead, k_right, blocks[1], right_part, masked[1]),
-        after=(left_one,),
-    )
-    right_one_ahead = passed_along(right_one, "site", -1)
-    left_part = call(
-        left_half, part, LEFT_SCRATCH, operands=(left_one, k_left, blocks[1]), after=(right_one,)
-    )
-    right_part = call(right_half, part, RIGHT_SCRATCH, operands=(right_one, k_right, blocks[0]))
+    right_part = call(
+        right_half, part, RIGHT_SCRATCH, operands=(right_one, k_right, blocks[0]), after=(left_one,)
+    )
+    left_part = call(left_half, part, LEFT_SCRATCH, operands=(left_one, k_left, blocks[1]))
+    right_out, right_far = call(
+        right_rest,
+        [flat, part],
+        RIGHT_SCRATCH,
+        operands=(right_one_ahead, k_right, blocks[0], right_part, masked[0]),
+        after=(left_part,),
+    )
+    right_got = shifted(right_out, "sector", -1)
     left_out, left_far = call(
         left_rest,
         [flat, part],
         LEFT_SCRATCH,
         operands=(left_one_behind, k_left, far_blocks[1], left_part, turned[1]),
-        after=(right_part,),
+        after=(right_out,),
     )
     left_got = shifted(left_out, "sector", 1)
-    right_out, right_far = call(
-        right_rest,
-        [flat, part],
-        RIGHT_SCRATCH,
-        operands=(right_one_ahead, k_right, blocks[0], right_part, masked[0]),
-        after=(left_out,),
-    )
-    right_got = shifted(right_out, "sector", -1)
     position = lax.axis_index("sector")
     first_flag = (position == 0).astype(jnp.int32).reshape(1)
     last_flag = (position == lax.axis_size("sector") - 1).astype(jnp.int32).reshape(1)
     diag = pltpu.VMEM((2, 128, HALF), BF)
-    first, first_sum = call(
+    raw = pltpu.VMEM((4, BLK, WB * BLK), BF)
+    devices = lax.axis_size("site")
+    own, away, second_sum = call(
+        second_body,
+        [shape((128, 256), F32), shape((128, 256), F32), shape((8, 128), F32)],
+        [raw, kept, diag, pltpu.SemaphoreType.DMA],
+        smem=1,
+        hbm=1,
+        operands=(last_flag, right_raw, right_got, left_part, left_far),
+        after=(left_out,),
+    )
+    back = passed_along(away, "site", -1)
+    first, sums = call(
         first_body,
-        [shape((256, 256), F32), shape((8, 128), F32)],
-        [diag],
+        [shape((256, 256), F32), shape((devices, 8, 128), F32)],
+        [raw, kept, diag, pltpu.SemaphoreType.DMA],
         smem=1,
-        operands=(first_flag, left_got, left_edge, right_part, right_far),
-        after=(right_out,),
-    )
-    devices = lax.axis_size("site")
-    own, away, sums = call(
-        second_body,
-        [shape((128, 256), F32), shape((128, 256), F32), shape((devices, 8, 128), F32)],
-        [diag],
-        smem=1,
-        operands=(last_flag, right_got, right_edge, left_part, left_far, first_sum),
-    )
-    back = passed_along(away, "site", -1)
+        hbm=1,
+        operands=(first_flag, left_raw, left_got, right_part, right_far, second_sum),
+    )
     gathered = lax.all_to_all(sums, "site", 0, 0, tiled=True)
     return call(
         functools.partial(final_body, 256 * 256 * devices),
-        shape((2, 4, BLK, 256), F32),
+        jax.ShapeDtypeStruct((2, 4, BLK, 256), F32),
         operands=(first, own, back, gathered),
     )
 

time: 69.7 us -> 66 us (0.947)
  the two profiles are of different devices: /device:TPU:199 before, /device:TPU:257 now
where the time goes in v2:
time: 66 us; the launch traced here: 65.7 us
  blocking collectives  18.6 us (28%)
  Pallas kernels  15.8 us (24%)
  waiting for transfers between devices  14.6 us (22%)
  starting transfers between devices  12.9 us (20%)
  local copies, waits for them, and re-layouts  3.63 us (6%)
    all_to_all x1, blocking collectives, local(): gathered = lax.all_to_all(sums, 'site', 0, 0, tiled=True)  18.6 us
    pallas_call x12, Pallas kernels, call(): pl.pallas_call(ordered, out_shape=outs, in_specs=[pl.BlockSpec(memory_spa...  15.8 us
    ppermute x2, waiting for transfers between devices, shifted(): return lax.ppermute(value, axis, pairs)  9.11 us
    ppermute x6, starting transfers between devices, passed_along(): return lax.ppermute(block, axis, route)  7.57 us
    ppermute x6, waiting for transfers between devices, passed_along(): return lax.ppermute(block, axis, route)  5.48 us
    ppermute x2, starting transfers between devices, shifted(): return lax.ppermute(value, axis, pairs)  5.37 us
    unnamed x16, local copies, waits for them, and re-layouts  3.24 us
  transfers between devices with their start and end apart: 8, of which 4 were waited for; matrix products, arithmetic and copies ran while one was open for 1% of the time, Pallas kernels for 23%

profile of v2, /device:TPU:257, one launch (start us, length us, event | category | flops | bytes accessed | tf_op | source)
XLA Modules:
  0.0 65.7 jit_solution(1532222435330398458)
XLA Ops:
  0.0 0.7 %collective-permute-start.2 = (bf16[4,64,1088]{2,1,0:T(8,128)(2,1)}, bf16[4,64,1088]{2,1,0:T(8,128)(2,1)S(1)}, u32[]{:S(2)}, u32[]{:S(2)}) collective-permute-start(bf16[4,64,1088]{2,1,0:T(8,128)(2,1)} %bitcast.26), channel_id=1, source_target_pairs={{0,480},{32,0},{64,32},{96,64},{128,96},{160,128},{192,160},{224,1... | collective-permute-start | bytes 1671176 | tf_op jit(solution)/shard_map/ppermute | solution.py:361
  0.7 0.0 copy-start.6
  0.7 0.0 copy-start.7
  0.7 1.2 %collective-permute-start = (bf16[4,64,1088]{2,1,0:T(8,128)(2,1)}, bf16[4,64,1088]{2,1,0:T(8,128)(2,1)S(1)}, u32[]{:S(2)}, u32[]{:S(2)}) collective-permute-start(bf16[4,64,1088]{2,1,0:T(8,128)(2,1)} %bitcast.29), channel_id=1, source_target_pairs={{0,32},{32,64},{64,96},{96,128},{128,160},{160,192},{192,224},{224... | collective-permute-start | bytes 1671176 | tf_op jit(solution)/shard_map/ppermute | solution.py:361
  1.9 1.1 %shard_map.73 = (bf16[2,256,256]{2,1,0:T(8,128)(2,1)S(1)}, bf16[2,256,128]{2,1,0:T(8,128)(2,1)S(1)}) custom-call(s32[2,4]{1,0:T(2,128)} %refs_0_.1, s32[2,4,4]{2,1,0:T(4,128)} %refs_1_.1, bf16[2,4,64,256]{3,2,1,0:T(8,128)(2,1)} %refs_2_.1), custom_call_target="tpu_custom_call" | custom-call | flops 1320000000 | bytes 1 | tf_op jit(solution)/shard_map/pallas_call | solution.py:43
  2.9 0.5 collective-permute-start.1
  3.5 0.0 copy-done.6
  3.5 0.0 copy-done.7
  3.5 0.1 reshape.18
  3.6 0.1 copy.11.refs_3_
  3.7 3.6 %shard_map.74 = (bf16[2,4,256,256]{3,2,1,0:T(8,128)(2,1)S(1)}, bf16[2,256,128]{2,1,0:T(8,128)(2,1)S(1)}, bf16[544,144]{1,0:T(8,128)(2,1)S(1)}, bf16[544,144]{1,0...) custom-call(bf16[4,64,1088]{2,1,0:T(8,128)(2,1)} %bitcast.30, ...), custom_call_target="tpu_custom_call" | custom-call | flops 1320000000 | bytes 1 | tf_op jit(solution)/shard_map/pallas_call | solution.py:43
  7.3 0.1 slice_bitcast_fusion
  7.4 2.5 %collective-permute-done.2.refs_0_ = bf16[4,64,1088]{2,1,0:T(8,128)(2,1)S(1)} collective-permute-done((bf16[4,64,1088]{2,1,0:T(8,128)(2,1)}, bf16[4,64,1088]{2,1,0:T(8,128)(2,1)S(1)}, u32[]{:S(2)}, u32[]{:S(2)}) %collective-permute-start.2) | collective-permute-done | bytes 557088 | tf_op jit(solution)/shard_map/ppermute | solution.py:361
  9.9 1.4 %shard_map.75.refs_2_.refs_5_.refs_0_ = bf16[64,4352]{1,0:T(8,128)(2,1)S(1)} custom-call(bf16[4,64,1088]{2,1,0:T(8,128)(2,1)S(1)} %collective-permute-done.2.refs_0_, bf16[544,144]{1,0:T(8,128)(2,1)S(1)} %get-tuple-element.28.refs_1_, bf16[4,256,256]{2,1,0:T(8,128)(2,1)S(1)} %get-tuple-element.44.refs_2_, bf16[128,4352]{1,0:T(8,128)(2,1)S(1)} %get-tuple-element.30.refs_3_, ...), custom_call_target="tpu_custom_call" | custom-call | flops 1320000000 | bytes 1 | tf_op jit(solution)/shard_map/pallas_call | solution.py:43
  11.3 1.4 %collective-permute-start.4 = (bf16[64,4352]{1,0:T(8,128)(2,1)S(1)}, bf16[64,4352]{1,0:T(8,128)(2,1)S(1)}, u32[]{:S(2)}, u32[]{:S(2)}) collective-permute-start(bf16[64,4352]{1,0:T(8,128)(2,1)S(1)} %shard_map.75.refs_2_.refs_5_.refs_0_), channel_id=1, source_target_pairs={{0,480},{32,0},{64,32},{96,64},{128,96},{160,128},{192,160},{224,1... | collective-permute-start | bytes 1671176 | tf_op jit(solution)/shard_map/ppermute | solution.py:361
  12.7 0.0 collective-permute-done.1.refs_0_
  12.7 0.0 collective-permute-done.refs_3_.refs_0_
  12.7 0.4 shard_map.76
  13.1 1.7 %shard_map.77.refs_0_.refs_3_ = bf16[64,4352]{1,0:T(8,128)(2,1)S(1)} custom-call(bf16[4,64,1088]{2,1,0:T(8,128)(2,1)S(1)} %collective-permute-done.refs_3_.refs_0_, bf16[544,144]{1,0:T(8,128)(2,1)S(1)} %get-tuple-element.25.refs_1_, bf16[2,256,256]{2,1,0:T(8,128)(2,1)S(1)} %get-tuple-element.46.refs_2_, ...), custom_call_target="tpu_custom_call" | custom-call | flops 1320000000 | bytes 1 | tf_op jit(solution)/shard_map/pallas_call | solution.py:43
  14.9 0.4 collective-permute-start.3
  15.3 1.1 %shard_map.78.refs_5_.refs_3_ = bf16[128,4352]{1,0:T(8,128)(2,1)S(1)} custom-call(bf16[64,4352]{1,0:T(8,128)(2,1)S(1)} %shard_map.77.refs_0_.refs_3_, bf16[544,144]{1,0:T(8,128)(2,1)S(1)} %get-tuple-element.25.refs_1_, bf16[4,256,256]{2,1,0:T(8,128)(2,1)S(1)} %get-tuple-element.44.refs_2_), custom_call_target="tpu_custom_call" | custom-call | flops 1320000000 | bytes 1 | tf_op jit(solution)/shard_map/pallas_call | solution.py:43
  16.4 0.9 %shard_map.79.refs_3_ = bf16[128,4352]{1,0:T(8,128)(2,1)S(1)} custom-call(bf16[64,4352]{1,0:T(8,128)(2,1)S(1)} %shard_map.75.refs_2_.refs_5_.refs_0_, bf16[544,144]{1,0:T(8,128)(2,1)S(1)} %get-tuple-element.28.refs_1_, bf16[4,256,256]{2,1,0:T(8,128)(2,1)S(1)} %get-tuple-element.43.refs_2_, bf16[64,4352]{1,0:T(8,128)(2,1)S(1)} %shard_map.77.refs_0_.refs_3_), custom_call_target="tpu_custom_call" | custom-call | flops 1320000000 | bytes 1 | tf_op jit(solution)/shard_map/pallas_call | solution.py:43
  17.3 0.0 copy-start.2
  17.3 3.0 %collective-permute-done.4.refs_0_ = bf16[64,4352]{1,0:T(8,128)(2,1)S(1)} collective-permute-done((bf16[64,4352]{1,0:T(8,128)(2,1)S(1)}, bf16[64,4352]{1,0:T(8,128)(2,1)S(1)}, u32[]{:S(2)}, u32[]{:S(2)}) %collective-permute-start.4) | collective-permute-done | bytes 557088 | tf_op jit(solution)/shard_map/ppermute | solution.py:361
  20.3 1.2 %shard_map.80 = (bf16[64,4352]{1,0:T(8,128)(2,1)S(1)}, bf16[128,4352]{1,0:T(8,128)(2,1)S(1)}) custom-call(bf16[64,4352]{1,0:T(8,128)(2,1)S(1)} %collective-permute-done.4.refs_0_, bf16[544,144]{1,0:T(8,128)(2,1)S(1)} %get-tuple-element.28.refs_1_, bf16[4,256,256]{2,1,0:T(8,128)(2,1)S(1)} %get-tuple-element.43.refs_2_, ...), custom_call_target="tpu_custom_call" | custom-call | flops 1320000000 | bytes 1 | tf_op jit(solution)/shard_map/pallas_call | solution.py:43
  21.5 0.0 copy-done.2
  21.5 0.0 copy-start.4
  21.5 1.0 %copy-done.4 = bf16[128,4352]{1,0:T(8,128)(2,1)} copy-done((bf16[128,4352]{1,0:T(8,128)(2,1)}, bf16[128,4352]{1,0:T(8,128)(2,1)S(1)}, u32[]{:S(2)}) %copy-start.4) | copy-done | bytes 1114136
  22.5 3.5 %collective-permute-start.6 = (bf16[64,4352]{1,0:T(8,128)(2,1)S(1)}, bf16[64,4352]{1,0:T(8,128)(2,1)S(1)}, u32[]{:S(2)}, u32[]{:S(2)}) collective-permute-start(bf16[64,4352]{1,0:T(8,128)(2,1)S(1)} %get-tuple-element.34.refs_5_), channel_id=1, source_target_pairs={{1,0},{2,1},{3,2},{4,3},{5,4},{6,5},{7,6},{8,7},{9,8},{10,9},{11,1... | collective-permute-start | bytes 1671176 | tf_op jit(solution)/shard_map/ppermute | solution.py:367
  25.9 0.0 collective-permute-done.3.refs_0_
  25.9 1.6 %shard_map.81 = (bf16[64,4352]{1,0:T(8,128)(2,1)S(1)}, bf16[128,4352]{1,0:T(8,128)(2,1)S(1)}) custom-call(bf16[64,4352]{1,0:T(8,128)(2,1)S(1)} %collective-permute-done.3.refs_0_, bf16[544,144]{1,0:T(8,128)(2,1)S(1)} %get-tuple-element.25.refs_1_, bf16[2,256,256]{2,1,0:T(8,128)(2,1)S(1)} %get-tuple-element.45.refs_2_, ...), custom_call_target="tpu_custom_call" | custom-call | flops 1320000000 | bytes 1 | tf_op jit(solution)/shard_map/pallas_call | solution.py:43
  27.5 0.0 copy-start
  27.6 1.0 %copy-done = bf16[128,4352]{1,0:T(8,128)(2,1)} copy-done((bf16[128,4352]{1,0:T(8,128)(2,1)}, bf16[128,4352]{1,0:T(8,128)(2,1)S(1)}, u32[]{:S(2)}) %copy-start) | copy-done | bytes 1114136
  28.6 1.9 %collective-permute-start.5 = (bf16[64,4352]{1,0:T(8,128)(2,1)S(1)}, bf16[64,4352]{1,0:T(8,128)(2,1)S(1)}, u32[]{:S(2)}, u32[]{:S(2)}) collective-permute-start(bf16[64,4352]{1,0:T(8,128)(2,1)S(1)} %get-tuple-element.35.refs_5_), channel_id=1, source_target_pairs={{0,1},{1,2},{2,3},{3,4},{4,5},{5,6},{6,7},{7,8},{8,9},{9,10},{10,1... | collective-permute-start | bytes 1671176 | tf_op jit(solution)/shard_map/ppermute | solution.py:367
  30.5 5.5 %collective-permute-done.6.refs_2_ = bf16[64,4352]{1,0:T(8,128)(2,1)S(1)} collective-permute-done((bf16[64,4352]{1,0:T(8,128)(2,1)S(1)}, bf16[64,4352]{1,0:T(8,128)(2,1)S(1)}, u32[]{:S(2)}, u32[]{:S(2)}) %collective-permute-start.6) | collective-permute-done | bytes 557088 | tf_op jit(solution)/shard_map/ppermute | solution.py:367
  36.0 0.0 copy-start.1
  36.0 1.2 %copy-done.1 = bf16[128,4352]{1,0:T(8,128)(2,1)S(1)} copy-done((bf16[128,4352]{1,0:T(8,128)(2,1)S(1)}, bf16[128,4352]{1,0:T(8,128)(2,1)}, u32[]{:S(2)}) %copy-start.1) | copy-done | bytes 1114136
  37.2 0.0 copy-start.3
  37.2 0.0 copy-start.5
  37.2 0.9 %shard_map.82 = (f32[128,256]{1,0:T(8,128)S(1)}, f32[128,256]{1,0:T(8,128)S(1)}, f32[8,128]{1,0:T(8,128)S(1)}) custom-call(s32[1]{0:T(128)} %bitcast.13.refs_0_, bf16[4,64,1088]{2,1,0:T(8,128)(2,1)} %bitcast.28, bf16[64,4352]{1,0:T(8,128)(2,1)S(1)} %collective-permute-done.6.refs_2_, bf16[128,4352]{1,0:T(8,128)(2,1)S(1)} %shard_map.78.refs_5_.refs_3_, ...), custom_call_target="tpu_custom_call" | custom-call | flops 1320000000 | bytes 1 | tf_op jit(solution)/shard_map/pallas_call | solution.py:43
  38.1 3.4 %collective-permute-start.7 = (f32[128,256]{1,0:T(8,128)S(1)}, f32[128,256]{1,0:T(8,128)S(1)}, u32[]{:S(2)}, u32[]{:S(2)}) collective-permute-start(f32[128,256]{1,0:T(8,128)S(1)} %get-tuple-element.41), channel_id=1, source_target_pairs={{0,480},{32,0},{64,32},{96,64},{128,96},{160,128},{192,160},{224,1... | collective-permute-start | bytes 393224 | tf_op jit(solution)/shard_map/ppermute | solution.py:361
  41.5 3.6 %collective-permute-done.5.refs_2_ = bf16[64,4352]{1,0:T(8,128)(2,1)S(1)} collective-permute-done((bf16[64,4352]{1,0:T(8,128)(2,1)S(1)}, bf16[64,4352]{1,0:T(8,128)(2,1)S(1)}, u32[]{:S(2)}, u32[]{:S(2)}) %collective-permute-start.5) | collective-permute-done | bytes 557088 | tf_op jit(solution)/shard_map/ppermute | solution.py:367
  45.1 0.0 copy-done.3
  45.1 0.0 copy-done.5
  45.1 1.1 %shard_map.83 = (f32[256,256]{1,0:T(8,128)S(1)}, f32[16,8,128]{2,1,0:T(8,128)S(1)}) custom-call(s32[1]{0:T(128)} %bitcast.refs_0_, bf16[4,64,1088]{2,1,0:T(8,128)(2,1)} %bitcast.31, bf16[64,4352]{1,0:T(8,128)(2,1)S(1)} %collective-permute-done.5.refs_2_, bf16[128,4352]{1,0:T(8,128)(2,1)S(1)} %copy-done.3, bf16[128,4352]{1,0:T(8,128)(2,1)S(1)} %copy-done.5, ...), custom_call_target="tpu_custom_call" | custom-call | flops 1320000000 | bytes 1 | tf_op jit(solution)/shard_map/pallas_call | solution.py:43
  46.2 18.6 %all_to_all.5.refs_3_ = f32[16,8,128]{2,1,0:T(8,128)S(1)} all-to-all(f32[16,8,128]{2,1,0:T(8,128)S(1)} %get-tuple-element.42), channel_id=1, replica_groups=mesh['site'=16,'sector'=32] {'site'}, dimensions={0} | all-to-all | bytes 131072 | tf_op jit(solution)/shard_map/all_to_all | solution.py:482
  64.8 0.0 collective-permute-done.7.refs_2_
  64.8 0.9 %shard_map.84 = f32[2,4,64,256]{3,2,1,0:T(8,128)} custom-call(f32[256,256]{1,0:T(8,128)S(1)} %get-tuple-element.39.refs_0_, f32[128,256]{1,0:T(8,128)S(1)} %get-tuple-element.40.refs_1_, f32[128,256]{1,0:T(8,128)S(1)} %collective-permute-done.7.refs_2_, f32[16,8,128]{2,1,0:T(8,128)S(1)} %all_to_all.5.refs_3_), custom_call_target="tpu_custom_call" | custom-call | flops 1320000000 | bytes 1 | tf_op jit(solution)/shard_map/pallas_call | solution.py:43
  (6 shorter events, 0.1 us)
Async XLA Ops:
  0.0 9.9 %collective-permute-start.2 = (bf16[4,64,1088]{2,1,0:T(8,128)(2,1)}, bf16[4,64,1088]{2,1,0:T(8,128)(2,1)S(1)}, u32[]{:S(2)}, u32[]{:S(2)}) collective-permute-start(bf16[4,64,1088]{2,1,0:T(8,128)(2,1)} %bitcast.26), channel_id=1, source_target_pairs={{0,480},{32,0},{64,32},{96,64},{128,96},{160,128},{192,160},{224,1... | collective-permute-start | bytes 1671176 | tf_op jit(solution)/shard_map/ppermute | solution.py:361
  0.7 2.8 %copy-start.6 = (s32[17,17,4]{1,2,0:T(4,128)S(1)}, s32[17,17,4]{1,2,0:T(4,128)}, u32[]{:S(2)}) copy-start(s32[17,17,4]{1,2,0:T(4,128)} %param.13) | copy-start | bytes 13876
  0.7 2.8 %copy-start.7 = (bf16[17,17,4]{1,2,0:T(4,128)(2,1)S(1)}, bf16[17,17,4]{1,2,0:T(4,128)(2,1)}, u32[]{:S(2)}) copy-start(bf16[17,17,4]{1,2,0:T(4,128)(2,1)} %param.12) | copy-start | bytes 6940
  0.7 12.0 %collective-permute-start = (bf16[4,64,1088]{2,1,0:T(8,128)(2,1)}, bf16[4,64,1088]{2,1,0:T(8,128)(2,1)S(1)}, u32[]{:S(2)}, u32[]{:S(2)}) collective-permute-start(bf16[4,64,1088]{2,1,0:T(8,128)(2,1)} %bitcast.29), channel_id=1, source_target_pairs={{0,32},{32,64},{64,96},{96,128},{128,160},{160,192},{192,224},{224... | collective-permute-start | bytes 1671176 | tf_op jit(solution)/shard_map/ppermute | solution.py:361
  2.9 9.7 %collective-permute-start.1 = (bf16[2,256,128]{2,1,0:T(8,128)(2,1)S(1)}, bf16[2,256,128]{2,1,0:T(8,128)(2,1)S(1)}, u32[]{:S(2)}, u32[]{:S(2)}) collective-permute-start(bf16[2,256,128]{2,1,0:T(8,128)(2,1)S(1)} %get-tuple-element.26), channel_id=1, source_target_pairs={{0,32},{32,64},{64,96},{96,128},{128,160},{160,192},{192,224},{224... | collective-permute-start | bytes 393224 | tf_op jit(solution)/shard_map/ppermute | solution.py:361
  11.3 9.0 %collective-permute-start.4 = (bf16[64,4352]{1,0:T(8,128)(2,1)S(1)}, bf16[64,4352]{1,0:T(8,128)(2,1)S(1)}, u32[]{:S(2)}, u32[]{:S(2)}) collective-permute-start(bf16[64,4352]{1,0:T(8,128)(2,1)S(1)} %shard_map.75.refs_2_.refs_5_.refs_0_), channel_id=1, source_target_pairs={{0,480},{32,0},{64,32},{96,64},{128,96},{160,128},{192,160},{224,1... | collective-permute-start | bytes 1671176 | tf_op jit(solution)/shard_map/ppermute | solution.py:361
  14.9 11.1 %collective-permute-start.3 = (bf16[64,4352]{1,0:T(8,128)(2,1)S(1)}, bf16[64,4352]{1,0:T(8,128)(2,1)S(1)}, u32[]{:S(2)}, u32[]{:S(2)}) collective-permute-start(bf16[64,4352]{1,0:T(8,128)(2,1)S(1)} %shard_map.77.refs_0_.refs_3_), channel_id=1, source_target_pairs={{0,32},{32,64},{64,96},{96,128},{128,160},{160,192},{192,224},{224... | collective-permute-start | bytes 1671176 | tf_op jit(solution)/shard_map/ppermute | solution.py:361
  17.3 4.2 %copy-start.2 = (bf16[128,4352]{1,0:T(8,128)(2,1)}, bf16[128,4352]{1,0:T(8,128)(2,1)S(1)}, u32[]{:S(2)}) copy-start(bf16[128,4352]{1,0:T(8,128)(2,1)S(1)} %shard_map.79.refs_3_) | copy-start | bytes 3342340
  21.5 1.0 %copy-start.4 = (bf16[128,4352]{1,0:T(8,128)(2,1)}, bf16[128,4352]{1,0:T(8,128)(2,1)S(1)}, u32[]{:S(2)}) copy-start(bf16[128,4352]{1,0:T(8,128)(2,1)S(1)} %get-tuple-element.36.refs_4_) | copy-start | bytes 3342340
  22.5 13.5 %collective-permute-start.6 = (bf16[64,4352]{1,0:T(8,128)(2,1)S(1)}, bf16[64,4352]{1,0:T(8,128)(2,1)S(1)}, u32[]{:S(2)}, u32[]{:S(2)}) collective-permute-start(bf16[64,4352]{1,0:T(8,128)(2,1)S(1)} %get-tuple-element.34.refs_5_), channel_id=1, source_target_pairs={{1,0},{2,1},{3,2},{4,3},{5,4},{6,5},{7,6},{8,7},{9,8},{10,9},{11,1... | collective-permute-start | bytes 1671176 | tf_op jit(solution)/shard_map/ppermute | solution.py:367
  27.5 1.0 %copy-start = (bf16[128,4352]{1,0:T(8,128)(2,1)}, bf16[128,4352]{1,0:T(8,128)(2,1)S(1)}, u32[]{:S(2)}) copy-start(bf16[128,4352]{1,0:T(8,128)(2,1)S(1)} %get-tuple-element.37.refs_4_) | copy-start | bytes 3342340
  28.6 16.6 %collective-permute-start.5 = (bf16[64,4352]{1,0:T(8,128)(2,1)S(1)}, bf16[64,4352]{1,0:T(8,128)(2,1)S(1)}, u32[]{:S(2)}, u32[]{:S(2)}) collective-permute-start(bf16[64,4352]{1,0:T(8,128)(2,1)S(1)} %get-tuple-element.35.refs_5_), channel_id=1, source_target_pairs={{0,1},{1,2},{2,3},{3,4},{4,5},{5,6},{6,7},{7,8},{8,9},{9,10},{10,1... | collective-permute-start | bytes 1671176 | tf_op jit(solution)/shard_map/ppermute | solution.py:367
  36.0 1.2 %copy-start.1 = (bf16[128,4352]{1,0:T(8,128)(2,1)S(1)}, bf16[128,4352]{1,0:T(8,128)(2,1)}, u32[]{:S(2)}) copy-start(bf16[128,4352]{1,0:T(8,128)(2,1)} %copy-done) | copy-start | bytes 3342340
  37.2 7.9 %copy-start.3 = (bf16[128,4352]{1,0:T(8,128)(2,1)S(1)}, bf16[128,4352]{1,0:T(8,128)(2,1)}, u32[]{:S(2)}) copy-start(bf16[128,4352]{1,0:T(8,128)(2,1)} %copy-done.2) | copy-start | bytes 3342340
  37.2 7.9 %copy-start.5 = (bf16[128,4352]{1,0:T(8,128)(2,1)S(1)}, bf16[128,4352]{1,0:T(8,128)(2,1)}, u32[]{:S(2)}) copy-start(bf16[128,4352]{1,0:T(8,128)(2,1)} %copy-done.4) | copy-start | bytes 3342340
  38.1 26.7 %collective-permute-start.7 = (f32[128,256]{1,0:T(8,128)S(1)}, f32[128,256]{1,0:T(8,128)S(1)}, u32[]{:S(2)}, u32[]{:S(2)}) collective-permute-start(f32[128,256]{1,0:T(8,128)S(1)} %get-tuple-element.41), channel_id=1, source_target_pairs={{0,480},{32,0},{64,32},{96,64},{128,96},{160,128},{192,160},{224,1... | collective-permute-start | bytes 393224 | tf_op jit(solution)/shard_map/ppermute | solution.py:361

commit v3 on v2

--- a/solution.py
+++ b/solution.py
@@ -243,6 +243,16 @@
 def right_half(flat_ref, k_ref, b_ref, y_ref, m_ref, f_ref):
     grouped(flat_ref, m_ref)
     right_states(m_ref, k_ref[: 2 * WB * 8], b_ref, 0, f_ref, y_ref, 0)
+
+
+def left_far_half(flat_ref, k_ref, b_ref, y_ref, e_ref, m_ref):
+    rows_of(flat_ref, e_ref)
+    left_states(e_ref, k_ref, 2, b_ref, 2, m_ref, y_ref, 0)
+
+
+def right_far_half(flat_ref, k_ref, b_ref, y_ref, m_ref, f_ref):
+    grouped(flat_ref, m_ref)
+    right_states(m_ref, k_ref[2 * WB * 8 :], b_ref, 2, f_ref, y_ref, 0)
 
 
 def left_rest_raw(env_ref, k_ref, b_ref, own_ref, lhs_ref, out_ref, flat_ref, y_ref, e_ref, m_ref):
@@ -439,22 +449,38 @@
         right_half, part, RIGHT_SCRATCH, operands=(right_one, k_right, blocks[0]), after=(left_one,)
     )
     left_part = call(left_half, part, LEFT_SCRATCH, operands=(left_one, k_left, blocks[1]))
-    right_out, right_far = call(
+    right_out = call(
         right_rest,
-        [flat, part],
-        RIGHT_SCRATCH,
+        flat,
+        [whole, *RIGHT_SCRATCH],
         operands=(right_one_ahead, k_right, blocks[0], right_part, masked[0]),
         after=(left_part,),
     )
     right_got = shifted(right_out, "sector", -1)
-    left_out, left_far = call(
+    right_far = call(
+        right_far_half,
+        part,
+        RIGHT_SCRATCH,
+        operands=(right_one_ahead, k_right, blocks[0]),
+        after=(right_out,),
+        us=0.9,
+    )
+    left_out = call(
         left_rest,
-        [flat, part],
+        flat,
+        [whole, *LEFT_SCRATCH],
+        operands=(left_one_behind, k_left, far_blocks[1], left_part, turned[1]),
+        after=(right_far,),
+    )
+    left_got = shifted(left_out, "sector", 1)
+    left_far = call(
+        left_far_half,
+        part,
         LEFT_SCRATCH,
-        operands=(left_one_behind, k_left, far_blocks[1], left_part, turned[1]),
-        after=(right_out,),
-    )
-    left_got = shifted(left_out, "sector", 1)
+        operands=(left_one_behind, k_left, far_blocks[1]),
+        after=(left_out,),
+        us=1.1,
+    )
     position = lax.axis_index("sector")
     first_flag = (position == 0).astype(jnp.int32).reshape(1)
     last_flag = (position == lax.axis_size("sector") - 1).astype(jnp.int32).reshape(1)

time: 66 us -> 65.1 us (0.986)
  local copies, waits for them, and re-layouts: 3.63 us -> 0.42 us
  Pallas kernels: 15.8 us -> 17.8 us
    unnamed x16, local copies, waits for them, and re-layouts: 3.24 us -> 0.03 us
    pallas_call x12 -> x14, Pallas kernels: 15.8 us -> 17.8 us  [call(): pl.pallas_call(ordered, out_shape=outs, in_specs=[pl.BlockSpec(memory_spa...]
  transfers between devices with their start and end apart: 8 -> 8, of which waited for: 4 -> 4; matrix products, arithmetic and copies ran while one was open for 1% -> 1% of each run, Pallas kernels for 23% -> 26%
where the time goes in v3:
time: 65.1 us; the launch traced here: 64.8 us
  blocking collectives  18.6 us (29%)
  Pallas kernels  17.8 us (27%)
  waiting for transfers between devices  14.7 us (23%)
  starting transfers between devices  13.1 us (20%)
    all_to_all x1, blocking collectives, local(): gathered = lax.all_to_all(sums, 'site', 0, 0, tiled=True)  18.6 us
    pallas_call x14, Pallas kernels, call(): pl.pallas_call(ordered, out_shape=outs, in_specs=[pl.BlockSpec(memory_spa...  17.8 us
    ppermute x2, waiting for transfers between devices, shifted(): return lax.ppermute(value, axis, pairs)  9.19 us
    ppermute x6, starting transfers between devices, passed_along(): return lax.ppermute(block, axis, route)  7.56 us
    ppermute x2, starting transfers between devices, shifted(): return lax.ppermute(value, axis, pairs)  5.57 us
    ppermute x6, waiting for transfers between devices, passed_along(): return lax.ppermute(block, axis, route)  5.47 us
  transfers between devices with their start and end apart: 8, of which 4 were waited for; matrix products, arithmetic and copies ran while one was open for 1% of the time, Pallas kernels for 26%

profile of v3, /device:TPU:257, one launch (start us, length us, event | category | flops | bytes accessed | tf_op | source)
XLA Modules:
  0.0 64.8 jit_solution(14068169611939656298)
XLA Ops:
  0.0 0.7 %collective-permute-start.2 = (bf16[4,64,1088]{2,1,0:T(8,128)(2,1)}, bf16[4,64,1088]{2,1,0:T(8,128)(2,1)S(1)}, u32[]{:S(2)}, u32[]{:S(2)}) collective-permute-start(bf16[4,64,1088]{2,1,0:T(8,128)(2,1)} %bitcast.26), channel_id=1, source_target_pairs={{0,480},{32,0},{64,32},{96,64},{128,96},{160,128},{192,160},{224,1... | collective-permute-start | bytes 1671176 | tf_op jit(solution)/shard_map/ppermute | solution.py:371
  0.7 0.0 copy-start.6
  0.7 0.0 copy-start.7
  0.7 1.2 %collective-permute-start = (bf16[4,64,1088]{2,1,0:T(8,128)(2,1)}, bf16[4,64,1088]{2,1,0:T(8,128)(2,1)S(1)}, u32[]{:S(2)}, u32[]{:S(2)}) collective-permute-start(bf16[4,64,1088]{2,1,0:T(8,128)(2,1)} %bitcast.29), channel_id=1, source_target_pairs={{0,32},{32,64},{64,96},{96,128},{128,160},{160,192},{192,224},{224... | collective-permute-start | bytes 1671176 | tf_op jit(solution)/shard_map/ppermute | solution.py:371
  1.9 1.1 %shard_map.73 = (bf16[2,256,256]{2,1,0:T(8,128)(2,1)S(1)}, bf16[2,256,128]{2,1,0:T(8,128)(2,1)S(1)}) custom-call(s32[2,4]{1,0:T(2,128)} %refs_0_.1, s32[2,4,4]{2,1,0:T(4,128)} %refs_1_.1, bf16[2,4,64,256]{3,2,1,0:T(8,128)(2,1)} %refs_2_.1), custom_call_target="tpu_custom_call" | custom-call | flops 1320000000 | bytes 1 | tf_op jit(solution)/shard_map/pallas_call | solution.py:43
  2.9 0.5 collective-permute-start.1
  3.5 0.0 copy-done.6
  3.5 0.0 copy-done.7
  3.5 0.1 reshape.18
  3.6 0.1 copy.11.refs_3_
  3.7 3.6 %shard_map.74 = (bf16[2,4,256,256]{3,2,1,0:T(8,128)(2,1)S(1)}, bf16[2,256,128]{2,1,0:T(8,128)(2,1)S(1)}, bf16[544,144]{1,0:T(8,128)(2,1)S(1)}, bf16[544,144]{1,0...) custom-call(bf16[4,64,1088]{2,1,0:T(8,128)(2,1)} %bitcast.30, ...), custom_call_target="tpu_custom_call" | custom-call | flops 1320000000 | bytes 1 | tf_op jit(solution)/shard_map/pallas_call | solution.py:43
  7.3 0.1 slice_bitcast_fusion
  7.4 2.5 %collective-permute-done.2.refs_0_ = bf16[4,64,1088]{2,1,0:T(8,128)(2,1)S(1)} collective-permute-done((bf16[4,64,1088]{2,1,0:T(8,128)(2,1)}, bf16[4,64,1088]{2,1,0:T(8,128)(2,1)S(1)}, u32[]{:S(2)}, u32[]{:S(2)}) %collective-permute-start.2) | collective-permute-done | bytes 557088 | tf_op jit(solution)/shard_map/ppermute | solution.py:371
  9.9 1.3 %shard_map.75.refs_2_.refs_5_.refs_0_ = bf16[64,4352]{1,0:T(8,128)(2,1)S(1)} custom-call(bf16[4,64,1088]{2,1,0:T(8,128)(2,1)S(1)} %collective-permute-done.2.refs_0_, bf16[544,144]{1,0:T(8,128)(2,1)S(1)} %get-tuple-element.24.refs_1_, bf16[4,256,256]{2,1,0:T(8,128)(2,1)S(1)} %get-tuple-element.36.refs_2_, bf16[128,4352]{1,0:T(8,128)(2,1)S(1)} %get-tuple-element.26.refs_3_, ...), custom_call_target="tpu_custom_call" | custom-call | flops 1320000000 | bytes 1 | tf_op jit(solution)/shard_map/pallas_call | solution.py:43
  11.3 1.4 %collective-permute-start.4 = (bf16[64,4352]{1,0:T(8,128)(2,1)S(1)}, bf16[64,4352]{1,0:T(8,128)(2,1)S(1)}, u32[]{:S(2)}, u32[]{:S(2)}) collective-permute-start(bf16[64,4352]{1,0:T(8,128)(2,1)S(1)} %shard_map.75.refs_2_.refs_5_.refs_0_), channel_id=1, source_target_pairs={{0,480},{32,0},{64,32},{96,64},{128,96},{160,128},{192,160},{224,1... | collective-permute-start | bytes 1671176 | tf_op jit(solution)/shard_map/ppermute | solution.py:371
  12.7 0.0 collective-permute-done.1.refs_0_
  12.7 0.0 collective-permute-done.refs_3_.refs_0_
  12.7 0.4 shard_map.76
  13.1 1.7 %shard_map.77.refs_0_.refs_3_ = bf16[64,4352]{1,0:T(8,128)(2,1)S(1)} custom-call(bf16[4,64,1088]{2,1,0:T(8,128)(2,1)S(1)} %collective-permute-done.refs_3_.refs_0_, bf16[544,144]{1,0:T(8,128)(2,1)S(1)} %get-tuple-element.21.refs_1_, bf16[2,256,256]{2,1,0:T(8,128)(2,1)S(1)} %get-tuple-element.38.refs_2_, ...), custom_call_target="tpu_custom_call" | custom-call | flops 1320000000 | bytes 1 | tf_op jit(solution)/shard_map/pallas_call | solution.py:43
  14.9 0.4 collective-permute-start.3
  15.3 1.1 %shard_map.78.refs_5_.refs_3_ = bf16[128,4352]{1,0:T(8,128)(2,1)S(1)} custom-call(bf16[64,4352]{1,0:T(8,128)(2,1)S(1)} %shard_map.77.refs_0_.refs_3_, bf16[544,144]{1,0:T(8,128)(2,1)S(1)} %get-tuple-element.21.refs_1_, bf16[4,256,256]{2,1,0:T(8,128)(2,1)S(1)} %get-tuple-element.36.refs_2_), custom_call_target="tpu_custom_call" | custom-call | flops 1320000000 | bytes 1 | tf_op jit(solution)/shard_map/pallas_call | solution.py:43
  16.4 0.0 copy-start.2
  16.4 0.9 %shard_map.79.refs_3_ = bf16[128,4352]{1,0:T(8,128)(2,1)S(1)} custom-call(bf16[64,4352]{1,0:T(8,128)(2,1)S(1)} %shard_map.75.refs_2_.refs_5_.refs_0_, bf16[544,144]{1,0:T(8,128)(2,1)S(1)} %get-tuple-element.24.refs_1_, bf16[4,256,256]{2,1,0:T(8,128)(2,1)S(1)} %get-tuple-element.35.refs_2_, bf16[64,4352]{1,0:T(8,128)(2,1)S(1)} %shard_map.77.refs_0_.refs_3_), custom_call_target="tpu_custom_call" | custom-call | flops 1320000000 | bytes 1 | tf_op jit(solution)/shard_map/pallas_call | solution.py:43
  17.3 0.0 copy-start
  17.3 3.0 %collective-permute-done.4.refs_0_ = bf16[64,4352]{1,0:T(8,128)(2,1)S(1)} collective-permute-done((bf16[64,4352]{1,0:T(8,128)(2,1)S(1)}, bf16[64,4352]{1,0:T(8,128)(2,1)S(1)}, u32[]{:S(2)}, u32[]{:S(2)}) %collective-permute-start.4) | collective-permute-done | bytes 557088 | tf_op jit(solution)/shard_map/ppermute | solution.py:371
  20.3 1.2 %shard_map.80.refs_3_ = bf16[64,4352]{1,0:T(8,128)(2,1)S(1)} custom-call(bf16[64,4352]{1,0:T(8,128)(2,1)S(1)} %collective-permute-done.4.refs_0_, bf16[544,144]{1,0:T(8,128)(2,1)S(1)} %get-tuple-element.24.refs_1_, bf16[4,256,256]{2,1,0:T(8,128)(2,1)S(1)} %get-tuple-element.35.refs_2_, bf16[128,4352]{1,0:T(8,128)(2,1)S(1)} %shard_map.79.refs_3_, ...), custom_call_target="tpu_custom_call" | custom-call | flops 1320000000 | bytes 1 | tf_op jit(solution)/shard_map/pallas_call | solution.py:43
  21.5 0.0 copy-done
  21.5 3.7 %collective-permute-start.6 = (bf16[64,4352]{1,0:T(8,128)(2,1)S(1)}, bf16[64,4352]{1,0:T(8,128)(2,1)S(1)}, u32[]{:S(2)}, u32[]{:S(2)}) collective-permute-start(bf16[64,4352]{1,0:T(8,128)(2,1)S(1)} %shard_map.80.refs_3_), channel_id=1, source_target_pairs={{1,0},{2,1},{3,2},{4,3},{5,4},{6,5},{7,6},{8,7},{9,8},{10,9},{11,1... | collective-permute-start | bytes 1671176 | tf_op jit(solution)/shard_map/ppermute | solution.py:377
  25.1 0.9 %shard_map.81.refs_5_.refs_4_ = bf16[128,4352]{1,0:T(8,128)(2,1)S(1)} custom-call(bf16[64,4352]{1,0:T(8,128)(2,1)S(1)} %collective-permute-done.4.refs_0_, bf16[544,144]{1,0:T(8,128)(2,1)S(1)} %get-tuple-element.24.refs_1_, bf16[4,256,256]{2,1,0:T(8,128)(2,1)S(1)} %get-tuple-element.35.refs_2_, bf16[64,4352]{1,0:T(8,128)(2,1)S(1)} %shard_map.80.refs_3_), custom_call_target="tpu_custom_call" | custom-call | flops 990000000 | bytes 1 | tf_op jit(solution)/shard_map/pallas_call | solution.py:43
  26.0 0.0 copy-start.4
  26.0 0.0 collective-permute-done.3.refs_0_
  26.0 0.0 copy-done.2
  26.0 1.6 %shard_map.82.refs_3_.refs_5_ = bf16[64,4352]{1,0:T(8,128)(2,1)S(1)} custom-call(bf16[64,4352]{1,0:T(8,128)(2,1)S(1)} %collective-permute-done.3.refs_0_, bf16[544,144]{1,0:T(8,128)(2,1)S(1)} %get-tuple-element.21.refs_1_, bf16[2,256,256]{2,1,0:T(8,128)(2,1)S(1)} %get-tuple-element.37.refs_2_, bf16[128,4352]{1,0:T(8,128)(2,1)S(1)} %shard_map.78.refs_5_.refs_3_, ...), custom_call_target="tpu_custom_call" | custom-call | flops 1320000000 | bytes 1 | tf_op jit(solution)/shard_map/pallas_call | solution.py:43
  27.6 0.0 copy-done.4
  27.6 1.9 %collective-permute-start.5 = (bf16[64,4352]{1,0:T(8,128)(2,1)S(1)}, bf16[64,4352]{1,0:T(8,128)(2,1)S(1)}, u32[]{:S(2)}, u32[]{:S(2)}) collective-permute-start(bf16[64,4352]{1,0:T(8,128)(2,1)S(1)} %shard_map.82.refs_3_.refs_5_), channel_id=1, source_target_pairs={{0,1},{1,2},{2,3},{3,4},{4,5},{5,6},{6,7},{7,8},{8,9},{9,10},{10,1... | collective-permute-start | bytes 1671176 | tf_op jit(solution)/shard_map/ppermute | solution.py:377
  29.6 0.0 copy-start.3
  29.6 1.1 %shard_map.83.refs_4_ = bf16[128,4352]{1,0:T(8,128)(2,1)S(1)} custom-call(bf16[64,4352]{1,0:T(8,128)(2,1)S(1)} %collective-permute-done.3.refs_0_, bf16[544,144]{1,0:T(8,128)(2,1)S(1)} %get-tuple-element.21.refs_1_, bf16[2,256,256]{2,1,0:T(8,128)(2,1)S(1)} %get-tuple-element.37.refs_2_, bf16[64,4352]{1,0:T(8,128)(2,1)S(1)} %shard_map.82.refs_3_.refs_5_), custom_call_target="tpu_custom_call" | custom-call | flops 1210000000 | bytes 1 | tf_op jit(solution)/shard_map/pallas_call | solution.py:43
  30.7 4.3 %collective-permute-done.6.refs_2_ = bf16[64,4352]{1,0:T(8,128)(2,1)S(1)} collective-permute-done((bf16[64,4352]{1,0:T(8,128)(2,1)S(1)}, bf16[64,4352]{1,0:T(8,128)(2,1)S(1)}, u32[]{:S(2)}, u32[]{:S(2)}) %collective-permute-start.6) | collective-permute-done | bytes 557088 | tf_op jit(solution)/shard_map/ppermute | solution.py:377
  35.0 0.0 copy-done.3
  35.0 0.0 copy-start.1
  35.0 0.0 copy-start.5
  35.0 0.9 %shard_map.84 = (f32[128,256]{1,0:T(8,128)S(1)}, f32[128,256]{1,0:T(8,128)S(1)}, f32[8,128]{1,0:T(8,128)S(1)}) custom-call(s32[1]{0:T(128)} %bitcast.13.refs_0_, bf16[4,64,1088]{2,1,0:T(8,128)(2,1)} %bitcast.28, bf16[64,4352]{1,0:T(8,128)(2,1)S(1)} %collective-permute-done.6.refs_2_, bf16[128,4352]{1,0:T(8,128)(2,1)S(1)} %copy-done.3, ...), custom_call_target="tpu_custom_call" | custom-call | flops 1320000000 | bytes 1 | tf_op jit(solution)/shard_map/pallas_call | solution.py:43
  35.9 3.4 %collective-permute-start.7 = (f32[128,256]{1,0:T(8,128)S(1)}, f32[128,256]{1,0:T(8,128)S(1)}, u32[]{:S(2)}, u32[]{:S(2)}) collective-permute-start(f32[128,256]{1,0:T(8,128)S(1)} %get-tuple-element.33), channel_id=1, source_target_pairs={{0,480},{32,0},{64,32},{96,64},{128,96},{160,128},{192,160},{224,1... | collective-permute-start | bytes 393224 | tf_op jit(solution)/shard_map/ppermute | solution.py:371
  39.3 4.9 %collective-permute-done.5.refs_2_ = bf16[64,4352]{1,0:T(8,128)(2,1)S(1)} collective-permute-done((bf16[64,4352]{1,0:T(8,128)(2,1)S(1)}, bf16[64,4352]{1,0:T(8,128)(2,1)S(1)}, u32[]{:S(2)}, u32[]{:S(2)}) %collective-permute-start.5) | collective-permute-done | bytes 557088 | tf_op jit(solution)/shard_map/ppermute | solution.py:377
  44.2 0.0 copy-done.1
  44.2 0.0 copy-done.5
  44.2 1.1 %shard_map.85 = (f32[256,256]{1,0:T(8,128)S(1)}, f32[16,8,128]{2,1,0:T(8,128)S(1)}) custom-call(s32[1]{0:T(128)} %bitcast.refs_0_, bf16[4,64,1088]{2,1,0:T(8,128)(2,1)} %bitcast.31, bf16[64,4352]{1,0:T(8,128)(2,1)S(1)} %collective-permute-done.5.refs_2_, bf16[128,4352]{1,0:T(8,128)(2,1)S(1)} %copy-done.1, bf16[128,4352]{1,0:T(8,128)(2,1)S(1)} %copy-done.5, ...), custom_call_target="tpu_custom_call" | custom-call | flops 1320000000 | bytes 1 | tf_op jit(solution)/shard_map/pallas_call | solution.py:43
  45.3 18.6 %all_to_all.5.refs_3_ = f32[16,8,128]{2,1,0:T(8,128)S(1)} all-to-all(f32[16,8,128]{2,1,0:T(8,128)S(1)} %get-tuple-element.34), channel_id=1, replica_groups=mesh['site'=16,'sector'=32] {'site'}, dimensions={0} | all-to-all | bytes 131072 | tf_op jit(solution)/shard_map/all_to_all | solution.py:508
  63.9 0.0 collective-permute-done.7.refs_2_
  63.9 0.9 %shard_map.86 = f32[2,4,64,256]{3,2,1,0:T(8,128)} custom-call(f32[256,256]{1,0:T(8,128)S(1)} %get-tuple-element.31.refs_0_, f32[128,256]{1,0:T(8,128)S(1)} %get-tuple-element.32.refs_1_, f32[128,256]{1,0:T(8,128)S(1)} %collective-permute-done.7.refs_2_, f32[16,8,128]{2,1,0:T(8,128)S(1)} %all_to_all.5.refs_3_), custom_call_target="tpu_custom_call" | custom-call | flops 1320000000 | bytes 1 | tf_op jit(solution)/shard_map/pallas_call | solution.py:43
  (6 shorter events, 0.1 us)
Async XLA Ops:
  0.0 9.9 %collective-permute-start.2 = (bf16[4,64,1088]{2,1,0:T(8,128)(2,1)}, bf16[4,64,1088]{2,1,0:T(8,128)(2,1)S(1)}, u32[]{:S(2)}, u32[]{:S(2)}) collective-permute-start(bf16[4,64,1088]{2,1,0:T(8,128)(2,1)} %bitcast.26), channel_id=1, source_target_pairs={{0,480},{32,0},{64,32},{96,64},{128,96},{160,128},{192,160},{224,1... | collective-permute-start | bytes 1671176 | tf_op jit(solution)/shard_map/ppermute | solution.py:371
  0.7 2.8 %copy-start.6 = (s32[17,17,4]{1,2,0:T(4,128)S(1)}, s32[17,17,4]{1,2,0:T(4,128)}, u32[]{:S(2)}) copy-start(s32[17,17,4]{1,2,0:T(4,128)} %param.13) | copy-start | bytes 13876
  0.7 2.8 %copy-start.7 = (bf16[17,17,4]{1,2,0:T(4,128)(2,1)S(1)}, bf16[17,17,4]{1,2,0:T(4,128)(2,1)}, u32[]{:S(2)}) copy-start(bf16[17,17,4]{1,2,0:T(4,128)(2,1)} %param.12) | copy-start | bytes 6940
  0.7 12.0 %collective-permute-start = (bf16[4,64,1088]{2,1,0:T(8,128)(2,1)}, bf16[4,64,1088]{2,1,0:T(8,128)(2,1)S(1)}, u32[]{:S(2)}, u32[]{:S(2)}) collective-permute-start(bf16[4,64,1088]{2,1,0:T(8,128)(2,1)} %bitcast.29), channel_id=1, source_target_pairs={{0,32},{32,64},{64,96},{96,128},{128,160},{160,192},{192,224},{224... | collective-permute-start | bytes 1671176 | tf_op jit(solution)/shard_map/ppermute | solution.py:371
  2.9 9.7 %collective-permute-start.1 = (bf16[2,256,128]{2,1,0:T(8,128)(2,1)S(1)}, bf16[2,256,128]{2,1,0:T(8,128)(2,1)S(1)}, u32[]{:S(2)}, u32[]{:S(2)}) collective-permute-start(bf16[2,256,128]{2,1,0:T(8,128)(2,1)S(1)} %get-tuple-element.22), channel_id=1, source_target_pairs={{0,32},{32,64},{64,96},{96,128},{128,160},{160,192},{192,224},{224... | collective-permute-start | bytes 393224 | tf_op jit(solution)/shard_map/ppermute | solution.py:371
  11.3 9.0 %collective-permute-start.4 = (bf16[64,4352]{1,0:T(8,128)(2,1)S(1)}, bf16[64,4352]{1,0:T(8,128)(2,1)S(1)}, u32[]{:S(2)}, u32[]{:S(2)}) collective-permute-start(bf16[64,4352]{1,0:T(8,128)(2,1)S(1)} %shard_map.75.refs_2_.refs_5_.refs_0_), channel_id=1, source_target_pairs={{0,480},{32,0},{64,32},{96,64},{128,96},{160,128},{192,160},{224,1... | collective-permute-start | bytes 1671176 | tf_op jit(solution)/shard_map/ppermute | solution.py:371
  14.9 11.1 %collective-permute-start.3 = (bf16[64,4352]{1,0:T(8,128)(2,1)S(1)}, bf16[64,4352]{1,0:T(8,128)(2,1)S(1)}, u32[]{:S(2)}, u32[]{:S(2)}) collective-permute-start(bf16[64,4352]{1,0:T(8,128)(2,1)S(1)} %shard_map.77.refs_0_.refs_3_), channel_id=1, source_target_pairs={{0,32},{32,64},{64,96},{96,128},{128,160},{160,192},{192,224},{224... | collective-permute-start | bytes 1671176 | tf_op jit(solution)/shard_map/ppermute | solution.py:371
  16.4 9.6 %copy-start.2 = (bf16[128,4352]{1,0:T(8,128)(2,1)}, bf16[128,4352]{1,0:T(8,128)(2,1)S(1)}, u32[]{:S(2)}) copy-start(bf16[128,4352]{1,0:T(8,128)(2,1)S(1)} %shard_map.78.refs_5_.refs_3_) | copy-start | bytes 3342340
  17.3 4.2 %copy-start = (bf16[128,4352]{1,0:T(8,128)(2,1)}, bf16[128,4352]{1,0:T(8,128)(2,1)S(1)}, u32[]{:S(2)}) copy-start(bf16[128,4352]{1,0:T(8,128)(2,1)S(1)} %shard_map.79.refs_3_) | copy-start | bytes 3342340
  21.5 13.5 %collective-permute-start.6 = (bf16[64,4352]{1,0:T(8,128)(2,1)S(1)}, bf16[64,4352]{1,0:T(8,128)(2,1)S(1)}, u32[]{:S(2)}, u32[]{:S(2)}) collective-permute-start(bf16[64,4352]{1,0:T(8,128)(2,1)S(1)} %shard_map.80.refs_3_), channel_id=1, source_target_pairs={{1,0},{2,1},{3,2},{4,3},{5,4},{6,5},{7,6},{8,7},{9,8},{10,9},{11,1... | collective-permute-start | bytes 1671176 | tf_op jit(solution)/shard_map/ppermute | solution.py:377
  26.0 1.6 %copy-start.4 = (bf16[128,4352]{1,0:T(8,128)(2,1)}, bf16[128,4352]{1,0:T(8,128)(2,1)S(1)}, u32[]{:S(2)}) copy-start(bf16[128,4352]{1,0:T(8,128)(2,1)S(1)} %shard_map.81.refs_5_.refs_4_) | copy-start | bytes 3342340
  27.6 16.6 %collective-permute-start.5 = (bf16[64,4352]{1,0:T(8,128)(2,1)S(1)}, bf16[64,4352]{1,0:T(8,128)(2,1)S(1)}, u32[]{:S(2)}, u32[]{:S(2)}) collective-permute-start(bf16[64,4352]{1,0:T(8,128)(2,1)S(1)} %shard_map.82.refs_3_.refs_5_), channel_id=1, source_target_pairs={{0,1},{1,2},{2,3},{3,4},{4,5},{5,6},{6,7},{7,8},{8,9},{9,10},{10,1... | collective-permute-start | bytes 1671176 | tf_op jit(solution)/shard_map/ppermute | solution.py:377
  29.6 5.4 %copy-start.3 = (bf16[128,4352]{1,0:T(8,128)(2,1)S(1)}, bf16[128,4352]{1,0:T(8,128)(2,1)}, u32[]{:S(2)}) copy-start(bf16[128,4352]{1,0:T(8,128)(2,1)} %copy-done.2) | copy-start | bytes 3342340
  35.0 9.2 %copy-start.1 = (bf16[128,4352]{1,0:T(8,128)(2,1)S(1)}, bf16[128,4352]{1,0:T(8,128)(2,1)}, u32[]{:S(2)}) copy-start(bf16[128,4352]{1,0:T(8,128)(2,1)} %copy-done) | copy-start | bytes 3342340
  35.0 9.2 %copy-start.5 = (bf16[128,4352]{1,0:T(8,128)(2,1)S(1)}, bf16[128,4352]{1,0:T(8,128)(2,1)}, u32[]{:S(2)}) copy-start(bf16[128,4352]{1,0:T(8,128)(2,1)} %copy-done.4) | copy-start | bytes 3342340
  35.9 28.0 %collective-permute-start.7 = (f32[128,256]{1,0:T(8,128)S(1)}, f32[128,256]{1,0:T(8,128)S(1)}, u32[]{:S(2)}, u32[]{:S(2)}) collective-permute-start(f32[128,256]{1,0:T(8,128)S(1)} %get-tuple-element.33), channel_id=1, source_target_pairs={{0,480},{32,0},{64,32},{96,64},{128,96},{160,128},{192,160},{224,1... | collective-permute-start | bytes 393224 | tf_op jit(solution)/shard_map/ppermute | solution.py:371

commit v4 on v3

--- a/solution.py
+++ b/solution.py
@@ -126,13 +126,12 @@
     enlarge(wr_ref[...], kr_ref)
 
 
-def far_ops_body(a_ref, own_ref, b_ref, at_ref):
-    for j in range(2):
-        values = a_ref[j].astype(F32)
-        for p in range(2):
-            b_ref[j, p] = spread(values[:, p * BLK : (p + 1) * BLK], p)
-        at_ref[j, :, :128] = own_ref[j]
-        at_ref[j, :, 128:] = flipped(values, 2)
+def far_ops_body(j, a_ref, own_ref, b_ref, at_ref):
+    values = a_ref[j].astype(F32)
+    for p in range(2):
+        b_ref[p] = spread(values[:, p * BLK : (p + 1) * BLK], p)
+    at_ref[:, :128] = own_ref[j]
+    at_ref[:, 128:] = flipped(values, 2)
 
 
 def raw_pair(ref, u, lt):
@@ -430,9 +429,10 @@
         after=(left_part,),
     )
     right_one_ahead = passed_along(right_one, "site", -1)
-    far_blocks, turned = call(
-        far_ops_body,
-        [shape((2, 2, 256, 256)), shape((2, 256, 256))],
+    far_outs = [shape((2, 256, 256)), shape((256, 256))]
+    first_far, first_turned = call(
+        functools.partial(far_ops_body, 0),
+        far_outs,
         operands=(high_behind, turned_own),
         after=(right_one, left_behind),
         us=0.4,
@@ -441,10 +441,17 @@
         left_rest_raw,
         flat,
         [kept, whole, *LEFT_SCRATCH],
-        operands=(left_behind, k_left, far_blocks[0], left_part, turned[0]),
+        operands=(left_behind, k_left, first_far, left_part, first_turned),
         after=(right_one,),
     )
     left_one_behind = passed_along(left_one, "site", 1)
+    second_far, second_turned = call(
+        functools.partial(far_ops_body, 1),
+        far_outs,
+        operands=(high_behind, turned_own),
+        after=(left_one,),
+        us=0.4,
+    )
     right_part = call(
         right_half, part, RIGHT_SCRATCH, operands=(right_one, k_right, blocks[0]), after=(left_one,)
     )
@@ -469,7 +476,7 @@
         left_rest,
         flat,
         [whole, *LEFT_SCRATCH],
-        operands=(left_one_behind, k_left, far_blocks[1], left_part, turned[1]),
+        operands=(left_one_behind, k_left, second_far, left_part, second_turned),
         after=(right_far,),
     )
     left_got = shifted(left_out, "sector", 1)
@@ -477,7 +484,7 @@
         left_far_half,
         part,
         LEFT_SCRATCH,
-        operands=(left_one_behind, k_left, far_blocks[1]),
+        operands=(left_one_behind, k_left, second_far),
         after=(left_out,),
         us=1.1,
     )

time: 65.1 us -> 65.9 us (1.012)
  local copies, waits for them, and re-layouts: 0.42 us -> 1.38 us
    unnamed x16, local copies, waits for them, and re-layouts: 0.03 us -> 1.05 us
    pallas_call x14 -> x15, Pallas kernels: 17.8 us -> 17.9 us  [call(): pl.pallas_call(ordered, out_shape=outs, in_specs=[pl.BlockSpec(memory_spa...]
where the time goes in v4:
time: 65.9 us; the launch traced here: 65.7 us
  blocking collectives  18.6 us (28%)
  Pallas kernels  17.9 us (27%)
  waiting for transfers between devices  14.5 us (22%)
  starting transfers between devices  13.1 us (20%)
  local copies, waits for them, and re-layouts  1.38 us (2%)
    all_to_all x1, blocking collectives, local(): gathered = lax.all_to_all(sums, 'site', 0, 0, tiled=True)  18.6 us
    pallas_call x15, Pallas kernels, call(): pl.pallas_call(ordered, out_shape=outs, in_specs=[pl.BlockSpec(memory_spa...  17.9 us
    ppermute x2, waiting for transfers between devices, shifted(): return lax.ppermute(value, axis, pairs)  9 us
    ppermute x6, starting transfers between devices, passed_along(): return lax.ppermute(block, axis, route)  7.55 us
    ppermute x2, starting transfers between devices, shifted(): return lax.ppermute(value, axis, pairs)  5.56 us
    ppermute x6, waiting for transfers between devices, passed_along(): return lax.ppermute(block, axis, route)  5.46 us
  transfers between devices with their start and end apart: 8, of which 4 were waited for; matrix products, arithmetic and copies ran while one was open for 1% of the time, Pallas kernels for 26%

profile of v4, /device:TPU:257, one launch (start us, length us, event | category | flops | bytes accessed | tf_op | source)
XLA Modules:
  0.0 65.7 jit_solution(12290196823597209453)
XLA Ops:
  0.0 0.7 %collective-permute-start.2 = (bf16[4,64,1088]{2,1,0:T(8,128)(2,1)}, bf16[4,64,1088]{2,1,0:T(8,128)(2,1)S(1)}, u32[]{:S(2)}, u32[]{:S(2)}) collective-permute-start(bf16[4,64,1088]{2,1,0:T(8,128)(2,1)} %bitcast.18), channel_id=1, source_target_pairs={{0,480},{32,0},{64,32},{96,64},{128,96},{160,128},{192,160},{224,1... | collective-permute-start | bytes 1671176 | tf_op jit(solution)/shard_map/ppermute | solution.py:370
  0.7 0.0 copy-start.6
  0.7 0.0 copy-start.7
  0.7 1.2 %collective-permute-start = (bf16[4,64,1088]{2,1,0:T(8,128)(2,1)}, bf16[4,64,1088]{2,1,0:T(8,128)(2,1)S(1)}, u32[]{:S(2)}, u32[]{:S(2)}) collective-permute-start(bf16[4,64,1088]{2,1,0:T(8,128)(2,1)} %bitcast.21), channel_id=1, source_target_pairs={{0,32},{32,64},{64,96},{96,128},{128,160},{160,192},{192,224},{224... | collective-permute-start | bytes 1671176 | tf_op jit(solution)/shard_map/ppermute | solution.py:370
  1.9 1.1 %shard_map.73 = (bf16[2,256,256]{2,1,0:T(8,128)(2,1)S(1)}, bf16[2,256,128]{2,1,0:T(8,128)(2,1)S(1)}) custom-call(s32[2,4]{1,0:T(2,128)} %refs_0_.1, s32[2,4,4]{2,1,0:T(4,128)} %refs_1_.1, bf16[2,4,64,256]{3,2,1,0:T(8,128)(2,1)} %refs_2_.1), custom_call_target="tpu_custom_call" | custom-call | flops 1320000000 | bytes 1 | tf_op jit(solution)/shard_map/pallas_call | solution.py:43
  2.9 0.5 collective-permute-start.1
  3.5 0.0 copy-done.6
  3.5 0.0 copy-done.7
  3.5 0.1 reshape.18
  3.6 0.1 copy.11.refs_3_
  3.8 3.6 %shard_map.74 = (bf16[2,4,256,256]{3,2,1,0:T(8,128)(2,1)S(1)}, bf16[2,256,128]{2,1,0:T(8,128)(2,1)S(1)}, bf16[544,144]{1,0:T(8,128)(2,1)S(1)}, bf16[544,144]{1,0...) custom-call(bf16[4,64,1088]{2,1,0:T(8,128)(2,1)} %bitcast.22, ...), custom_call_target="tpu_custom_call" | custom-call | flops 1320000000 | bytes 1 | tf_op jit(solution)/shard_map/pallas_call | solution.py:43
  7.4 0.1 slice_bitcast_fusion
  7.4 2.5 %collective-permute-done.2.refs_0_ = bf16[4,64,1088]{2,1,0:T(8,128)(2,1)S(1)} collective-permute-done((bf16[4,64,1088]{2,1,0:T(8,128)(2,1)}, bf16[4,64,1088]{2,1,0:T(8,128)(2,1)S(1)}, u32[]{:S(2)}, u32[]{:S(2)}) %collective-permute-start.2) | collective-permute-done | bytes 557088 | tf_op jit(solution)/shard_map/ppermute | solution.py:370
  9.9 1.4 %shard_map.75.refs_2_.refs_5_.refs_0_ = bf16[64,4352]{1,0:T(8,128)(2,1)S(1)} custom-call(bf16[4,64,1088]{2,1,0:T(8,128)(2,1)S(1)} %collective-permute-done.2.refs_0_, bf16[544,144]{1,0:T(8,128)(2,1)S(1)} %get-tuple-element.26.refs_1_, bf16[4,256,256]{2,1,0:T(8,128)(2,1)S(1)} %get-tuple-element.40.refs_2_, bf16[128,4352]{1,0:T(8,128)(2,1)S(1)} %get-tuple-element.28.refs_3_, ...), custom_call_target="tpu_custom_call" | custom-call | flops 1320000000 | bytes 1 | tf_op jit(solution)/shard_map/pallas_call | solution.py:43
  11.3 1.4 %collective-permute-start.4 = (bf16[64,4352]{1,0:T(8,128)(2,1)S(1)}, bf16[64,4352]{1,0:T(8,128)(2,1)S(1)}, u32[]{:S(2)}, u32[]{:S(2)}) collective-permute-start(bf16[64,4352]{1,0:T(8,128)(2,1)S(1)} %shard_map.75.refs_2_.refs_5_.refs_0_), channel_id=1, source_target_pairs={{0,480},{32,0},{64,32},{96,64},{128,96},{160,128},{192,160},{224,1... | collective-permute-start | bytes 1671176 | tf_op jit(solution)/shard_map/ppermute | solution.py:370
  12.7 0.0 collective-permute-done.1.refs_0_
  12.7 0.0 collective-permute-done.refs_3_.refs_0_
  12.7 0.2 shard_map.76
  12.9 1.7 %shard_map.77.refs_2_.refs_0_.refs_3_ = bf16[64,4352]{1,0:T(8,128)(2,1)S(1)} custom-call(bf16[4,64,1088]{2,1,0:T(8,128)(2,1)S(1)} %collective-permute-done.refs_3_.refs_0_, bf16[544,144]{1,0:T(8,128)(2,1)S(1)} %get-tuple-element.23.refs_1_, bf16[2,256,256]{2,1,0:T(8,128)(2,1)S(1)} %get-tuple-element.30.refs_2_, ...), custom_call_target="tpu_custom_call" | custom-call | flops 1320000000 | bytes 1 | tf_op jit(solution)/shard_map/pallas_call | solution.py:43
  14.7 0.4 collective-permute-start.3
  15.0 0.2 shard_map.78
  15.3 1.1 %shard_map.79.refs_5_.refs_3_ = bf16[128,4352]{1,0:T(8,128)(2,1)S(1)} custom-call(bf16[64,4352]{1,0:T(8,128)(2,1)S(1)} %shard_map.77.refs_2_.refs_0_.refs_3_, bf16[544,144]{1,0:T(8,128)(2,1)S(1)} %get-tuple-element.23.refs_1_, bf16[4,256,256]{2,1,0:T(8,128)(2,1)S(1)} %get-tuple-element.40.refs_2_), custom_call_target="tpu_custom_call" | custom-call | flops 1320000000 | bytes 1 | tf_op jit(solution)/shard_map/pallas_call | solution.py:43
  16.4 0.0 copy-start.2
  16.4 0.9 %shard_map.80.refs_3_ = bf16[128,4352]{1,0:T(8,128)(2,1)S(1)} custom-call(bf16[64,4352]{1,0:T(8,128)(2,1)S(1)} %shard_map.75.refs_2_.refs_5_.refs_0_, bf16[544,144]{1,0:T(8,128)(2,1)S(1)} %get-tuple-element.26.refs_1_, bf16[4,256,256]{2,1,0:T(8,128)(2,1)S(1)} %get-tuple-element.39.refs_2_, bf16[64,4352]{1,0:T(8,128)(2,1)S(1)} %shard_map.77.refs_2_.refs_0_.refs_3_), custom_call_target="tpu_custom_call" | custom-call | flops 1320000000 | bytes 1 | tf_op jit(solution)/shard_map/pallas_call | solution.py:43
  17.3 3.0 %collective-permute-done.4.refs_0_ = bf16[64,4352]{1,0:T(8,128)(2,1)S(1)} collective-permute-done((bf16[64,4352]{1,0:T(8,128)(2,1)S(1)}, bf16[64,4352]{1,0:T(8,128)(2,1)S(1)}, u32[]{:S(2)}, u32[]{:S(2)}) %collective-permute-start.4) | collective-permute-done | bytes 557088 | tf_op jit(solution)/shard_map/ppermute | solution.py:370
  20.3 1.2 %shard_map.81.refs_3_ = bf16[64,4352]{1,0:T(8,128)(2,1)S(1)} custom-call(bf16[64,4352]{1,0:T(8,128)(2,1)S(1)} %collective-permute-done.4.refs_0_, bf16[544,144]{1,0:T(8,128)(2,1)S(1)} %get-tuple-element.26.refs_1_, bf16[4,256,256]{2,1,0:T(8,128)(2,1)S(1)} %get-tuple-element.39.refs_2_, bf16[128,4352]{1,0:T(8,128)(2,1)S(1)} %shard_map.80.refs_3_, ...), custom_call_target="tpu_custom_call" | custom-call | flops 1320000000 | bytes 1 | tf_op jit(solution)/shard_map/pallas_call | solution.py:43
  21.5 0.0 copy-start
  21.5 1.0 %copy-done = bf16[128,4352]{1,0:T(8,128)(2,1)} copy-done((bf16[128,4352]{1,0:T(8,128)(2,1)}, bf16[128,4352]{1,0:T(8,128)(2,1)S(1)}, u32[]{:S(2)}) %copy-start) | copy-done | bytes 1114136
  22.5 3.5 %collective-permute-start.6 = (bf16[64,4352]{1,0:T(8,128)(2,1)S(1)}, bf16[64,4352]{1,0:T(8,128)(2,1)S(1)}, u32[]{:S(2)}, u32[]{:S(2)}) collective-permute-start(bf16[64,4352]{1,0:T(8,128)(2,1)S(1)} %shard_map.81.refs_3_), channel_id=1, source_target_pairs={{1,0},{2,1},{3,2},{4,3},{5,4},{6,5},{7,6},{8,7},{9,8},{10,9},{11,1... | collective-permute-start | bytes 1671176 | tf_op jit(solution)/shard_map/ppermute | solution.py:376
  26.0 0.9 %shard_map.82.refs_5_.refs_4_ = bf16[128,4352]{1,0:T(8,128)(2,1)S(1)} custom-call(bf16[64,4352]{1,0:T(8,128)(2,1)S(1)} %collective-permute-done.4.refs_0_, bf16[544,144]{1,0:T(8,128)(2,1)S(1)} %get-tuple-element.26.refs_1_, bf16[4,256,256]{2,1,0:T(8,128)(2,1)S(1)} %get-tuple-element.39.refs_2_, bf16[64,4352]{1,0:T(8,128)(2,1)S(1)} %shard_map.81.refs_3_), custom_call_target="tpu_custom_call" | custom-call | flops 990000000 | bytes 1 | tf_op jit(solution)/shard_map/pallas_call | solution.py:43
  26.8 0.0 copy-start.4
  26.9 0.0 collective-permute-done.3.refs_0_
  26.9 0.0 copy-done.2
  26.9 1.6 %shard_map.83.refs_3_.refs_5_ = bf16[64,4352]{1,0:T(8,128)(2,1)S(1)} custom-call(bf16[64,4352]{1,0:T(8,128)(2,1)S(1)} %collective-permute-done.3.refs_0_, bf16[544,144]{1,0:T(8,128)(2,1)S(1)} %get-tuple-element.23.refs_1_, bf16[2,256,256]{2,1,0:T(8,128)(2,1)S(1)} %get-tuple-element.32.refs_2_, bf16[128,4352]{1,0:T(8,128)(2,1)S(1)} %shard_map.79.refs_5_.refs_3_, ...), custom_call_target="tpu_custom_call" | custom-call | flops 1320000000 | bytes 1 | tf_op jit(solution)/shard_map/pallas_call | solution.py:43
  28.5 0.0 copy-done.4
  28.5 2.1 %collective-permute-start.5 = (bf16[64,4352]{1,0:T(8,128)(2,1)S(1)}, bf16[64,4352]{1,0:T(8,128)(2,1)S(1)}, u32[]{:S(2)}, u32[]{:S(2)}) collective-permute-start(bf16[64,4352]{1,0:T(8,128)(2,1)S(1)} %shard_map.83.refs_3_.refs_5_), channel_id=1, source_target_pairs={{0,1},{1,2},{2,3},{3,4},{4,5},{5,6},{6,7},{7,8},{8,9},{9,10},{10,1... | collective-permute-start | bytes 1671176 | tf_op jit(solution)/shard_map/ppermute | solution.py:376
  30.6 0.0 copy-start.3
  30.6 1.1 %shard_map.84.refs_4_ = bf16[128,4352]{1,0:T(8,128)(2,1)S(1)} custom-call(bf16[64,4352]{1,0:T(8,128)(2,1)S(1)} %collective-permute-done.3.refs_0_, bf16[544,144]{1,0:T(8,128)(2,1)S(1)} %get-tuple-element.23.refs_1_, bf16[2,256,256]{2,1,0:T(8,128)(2,1)S(1)} %get-tuple-element.32.refs_2_, bf16[64,4352]{1,0:T(8,128)(2,1)S(1)} %shard_map.83.refs_3_.refs_5_), custom_call_target="tpu_custom_call" | custom-call | flops 1210000000 | bytes 1 | tf_op jit(solution)/shard_map/pallas_call | solution.py:43
  31.8 4.3 %collective-permute-done.6.refs_2_ = bf16[64,4352]{1,0:T(8,128)(2,1)S(1)} collective-permute-done((bf16[64,4352]{1,0:T(8,128)(2,1)S(1)}, bf16[64,4352]{1,0:T(8,128)(2,1)S(1)}, u32[]{:S(2)}, u32[]{:S(2)}) %collective-permute-start.6) | collective-permute-done | bytes 557088 | tf_op jit(solution)/shard_map/ppermute | solution.py:376
  36.0 0.0 copy-done.3
  36.0 0.0 copy-start.1
  36.0 0.0 copy-start.5
  36.0 0.9 %shard_map.85 = (f32[128,256]{1,0:T(8,128)S(1)}, f32[128,256]{1,0:T(8,128)S(1)}, f32[8,128]{1,0:T(8,128)S(1)}) custom-call(s32[1]{0:T(128)} %bitcast.9.refs_0_, bf16[4,64,1088]{2,1,0:T(8,128)(2,1)} %bitcast.20, bf16[64,4352]{1,0:T(8,128)(2,1)S(1)} %collective-permute-done.6.refs_2_, bf16[128,4352]{1,0:T(8,128)(2,1)S(1)} %copy-done.3, ...), custom_call_target="tpu_custom_call" | custom-call | flops 1320000000 | bytes 1 | tf_op jit(solution)/shard_map/pallas_call | solution.py:43
  36.9 3.4 %collective-permute-start.7 = (f32[128,256]{1,0:T(8,128)S(1)}, f32[128,256]{1,0:T(8,128)S(1)}, u32[]{:S(2)}, u32[]{:S(2)}) collective-permute-start(f32[128,256]{1,0:T(8,128)S(1)} %get-tuple-element.37), channel_id=1, source_target_pairs={{0,480},{32,0},{64,32},{96,64},{128,96},{160,128},{192,160},{224,1... | collective-permute-start | bytes 393224 | tf_op jit(solution)/shard_map/ppermute | solution.py:370
  40.3 4.7 %collective-permute-done.5.refs_2_ = bf16[64,4352]{1,0:T(8,128)(2,1)S(1)} collective-permute-done((bf16[64,4352]{1,0:T(8,128)(2,1)S(1)}, bf16[64,4352]{1,0:T(8,128)(2,1)S(1)}, u32[]{:S(2)}, u32[]{:S(2)}) %collective-permute-start.5) | collective-permute-done | bytes 557088 | tf_op jit(solution)/shard_map/ppermute | solution.py:376
  45.1 0.0 copy-done.1
  45.1 0.0 copy-done.5
  45.1 1.1 %shard_map.86 = (f32[256,256]{1,0:T(8,128)S(1)}, f32[16,8,128]{2,1,0:T(8,128)S(1)}) custom-call(s32[1]{0:T(128)} %bitcast.refs_0_, bf16[4,64,1088]{2,1,0:T(8,128)(2,1)} %bitcast.23, bf16[64,4352]{1,0:T(8,128)(2,1)S(1)} %collective-permute-done.5.refs_2_, bf16[128,4352]{1,0:T(8,128)(2,1)S(1)} %copy-done.1, bf16[128,4352]{1,0:T(8,128)(2,1)S(1)} %copy-done.5, ...), custom_call_target="tpu_custom_call" | custom-call | flops 1320000000 | bytes 1 | tf_op jit(solution)/shard_map/pallas_call | solution.py:43
  46.1 18.6 %all_to_all.5.refs_3_ = f32[16,8,128]{2,1,0:T(8,128)S(1)} all-to-all(f32[16,8,128]{2,1,0:T(8,128)S(1)} %get-tuple-element.38), channel_id=1, replica_groups=mesh['site'=16,'sector'=32] {'site'}, dimensions={0} | all-to-all | bytes 131072 | tf_op jit(solution)/shard_map/all_to_all | solution.py:515
  64.7 0.0 collective-permute-done.7.refs_2_
  64.7 0.9 %shard_map.87 = f32[2,4,64,256]{3,2,1,0:T(8,128)} custom-call(f32[256,256]{1,0:T(8,128)S(1)} %get-tuple-element.35.refs_0_, f32[128,256]{1,0:T(8,128)S(1)} %get-tuple-element.36.refs_1_, f32[128,256]{1,0:T(8,128)S(1)} %collective-permute-done.7.refs_2_, f32[16,8,128]{2,1,0:T(8,128)S(1)} %all_to_all.5.refs_3_), custom_call_target="tpu_custom_call" | custom-call | flops 1320000000 | bytes 1 | tf_op jit(solution)/shard_map/pallas_call | solution.py:43
  (4 shorter events, 0.1 us)
Async XLA Ops:
  0.0 9.9 %collective-permute-start.2 = (bf16[4,64,1088]{2,1,0:T(8,128)(2,1)}, bf16[4,64,1088]{2,1,0:T(8,128)(2,1)S(1)}, u32[]{:S(2)}, u32[]{:S(2)}) collective-permute-start(bf16[4,64,1088]{2,1,0:T(8,128)(2,1)} %bitcast.18), channel_id=1, source_target_pairs={{0,480},{32,0},{64,32},{96,64},{128,96},{160,128},{192,160},{224,1... | collective-permute-start | bytes 1671176 | tf_op jit(solution)/shard_map/ppermute | solution.py:370
  0.7 2.8 %copy-start.6 = (s32[17,17,4]{1,2,0:T(4,128)S(1)}, s32[17,17,4]{1,2,0:T(4,128)}, u32[]{:S(2)}) copy-start(s32[17,17,4]{1,2,0:T(4,128)} %param.13) | copy-start | bytes 13876
  0.7 2.8 %copy-start.7 = (bf16[17,17,4]{1,2,0:T(4,128)(2,1)S(1)}, bf16[17,17,4]{1,2,0:T(4,128)(2,1)}, u32[]{:S(2)}) copy-start(bf16[17,17,4]{1,2,0:T(4,128)(2,1)} %param.12) | copy-start | bytes 6940
  0.7 12.0 %collective-permute-start = (bf16[4,64,1088]{2,1,0:T(8,128)(2,1)}, bf16[4,64,1088]{2,1,0:T(8,128)(2,1)S(1)}, u32[]{:S(2)}, u32[]{:S(2)}) collective-permute-start(bf16[4,64,1088]{2,1,0:T(8,128)(2,1)} %bitcast.21), channel_id=1, source_target_pairs={{0,32},{32,64},{64,96},{96,128},{128,160},{160,192},{192,224},{224... | collective-permute-start | bytes 1671176 | tf_op jit(solution)/shard_map/ppermute | solution.py:370
  2.9 9.7 %collective-permute-start.1 = (bf16[2,256,128]{2,1,0:T(8,128)(2,1)S(1)}, bf16[2,256,128]{2,1,0:T(8,128)(2,1)S(1)}, u32[]{:S(2)}, u32[]{:S(2)}) collective-permute-start(bf16[2,256,128]{2,1,0:T(8,128)(2,1)S(1)} %get-tuple-element.24), channel_id=1, source_target_pairs={{0,32},{32,64},{64,96},{96,128},{128,160},{160,192},{192,224},{224... | collective-permute-start | bytes 393224 | tf_op jit(solution)/shard_map/ppermute | solution.py:370
  11.3 9.0 %collective-permute-start.4 = (bf16[64,4352]{1,0:T(8,128)(2,1)S(1)}, bf16[64,4352]{1,0:T(8,128)(2,1)S(1)}, u32[]{:S(2)}, u32[]{:S(2)}) collective-permute-start(bf16[64,4352]{1,0:T(8,128)(2,1)S(1)} %shard_map.75.refs_2_.refs_5_.refs_0_), channel_id=1, source_target_pairs={{0,480},{32,0},{64,32},{96,64},{128,96},{160,128},{192,160},{224,1... | collective-permute-start | bytes 1671176 | tf_op jit(solution)/shard_map/ppermute | solution.py:370
  14.7 12.2 %collective-permute-start.3 = (bf16[64,4352]{1,0:T(8,128)(2,1)S(1)}, bf16[64,4352]{1,0:T(8,128)(2,1)S(1)}, u32[]{:S(2)}, u32[]{:S(2)}) collective-permute-start(bf16[64,4352]{1,0:T(8,128)(2,1)S(1)} %shard_map.77.refs_2_.refs_0_.refs_3_), channel_id=1, source_target_pairs={{0,32},{32,64},{64,96},{96,128},{128,160},{160,192},{192,224},{224... | collective-permute-start | bytes 1671176 | tf_op jit(solution)/shard_map/ppermute | solution.py:370
  16.4 10.4 %copy-start.2 = (bf16[128,4352]{1,0:T(8,128)(2,1)}, bf16[128,4352]{1,0:T(8,128)(2,1)S(1)}, u32[]{:S(2)}) copy-start(bf16[128,4352]{1,0:T(8,128)(2,1)S(1)} %shard_map.79.refs_5_.refs_3_) | copy-start | bytes 3342340
  21.5 1.0 %copy-start = (bf16[128,4352]{1,0:T(8,128)(2,1)}, bf16[128,4352]{1,0:T(8,128)(2,1)S(1)}, u32[]{:S(2)}) copy-start(bf16[128,4352]{1,0:T(8,128)(2,1)S(1)} %shard_map.80.refs_3_) | copy-start | bytes 3342340
  22.5 13.5 %collective-permute-start.6 = (bf16[64,4352]{1,0:T(8,128)(2,1)S(1)}, bf16[64,4352]{1,0:T(8,128)(2,1)S(1)}, u32[]{:S(2)}, u32[]{:S(2)}) collective-permute-start(bf16[64,4352]{1,0:T(8,128)(2,1)S(1)} %shard_map.81.refs_3_), channel_id=1, source_target_pairs={{1,0},{2,1},{3,2},{4,3},{5,4},{6,5},{7,6},{8,7},{9,8},{10,9},{11,1... | collective-permute-start | bytes 1671176 | tf_op jit(solution)/shard_map/ppermute | solution.py:376
  26.8 1.6 %copy-start.4 = (bf16[128,4352]{1,0:T(8,128)(2,1)}, bf16[128,4352]{1,0:T(8,128)(2,1)S(1)}, u32[]{:S(2)}) copy-start(bf16[128,4352]{1,0:T(8,128)(2,1)S(1)} %shard_map.82.refs_5_.refs_4_) | copy-start | bytes 3342340
  28.5 16.6 %collective-permute-start.5 = (bf16[64,4352]{1,0:T(8,128)(2,1)S(1)}, bf16[64,4352]{1,0:T(8,128)(2,1)S(1)}, u32[]{:S(2)}, u32[]{:S(2)}) collective-permute-start(bf16[64,4352]{1,0:T(8,128)(2,1)S(1)} %shard_map.83.refs_3_.refs_5_), channel_id=1, source_target_pairs={{0,1},{1,2},{2,3},{3,4},{4,5},{5,6},{6,7},{7,8},{8,9},{9,10},{10,1... | collective-permute-start | bytes 1671176 | tf_op jit(solution)/shard_map/ppermute | solution.py:376
  30.6 5.4 %copy-start.3 = (bf16[128,4352]{1,0:T(8,128)(2,1)S(1)}, bf16[128,4352]{1,0:T(8,128)(2,1)}, u32[]{:S(2)}) copy-start(bf16[128,4352]{1,0:T(8,128)(2,1)} %copy-done.2) | copy-start | bytes 3342340
  36.0 9.0 %copy-start.1 = (bf16[128,4352]{1,0:T(8,128)(2,1)S(1)}, bf16[128,4352]{1,0:T(8,128)(2,1)}, u32[]{:S(2)}) copy-start(bf16[128,4352]{1,0:T(8,128)(2,1)} %copy-done) | copy-start | bytes 3342340
  36.0 9.0 %copy-start.5 = (bf16[128,4352]{1,0:T(8,128)(2,1)S(1)}, bf16[128,4352]{1,0:T(8,128)(2,1)}, u32[]{:S(2)}) copy-start(bf16[128,4352]{1,0:T(8,128)(2,1)} %copy-done.4) | copy-start | bytes 3342340
  36.9 27.8 %collective-permute-start.7 = (f32[128,256]{1,0:T(8,128)S(1)}, f32[128,256]{1,0:T(8,128)S(1)}, u32[]{:S(2)}, u32[]{:S(2)}) collective-permute-start(f32[128,256]{1,0:T(8,128)S(1)} %get-tuple-element.37), channel_id=1, source_target_pairs={{0,480},{32,0},{64,32},{96,64},{128,96},{160,128},{192,160},{224,1... | collective-permute-start | bytes 393224 | tf_op jit(solution)/shard_map/ppermute | solution.py:370
